TPU v7x, 32 devices: a whole 2x2x4 slice. The times are simulated.
32 devices in a mesh: mod: 2 (over core), seq: 4 (over z), tp: 4 (over y, x).
Axes of the slice: x: 2, y: 2, z: 4, core: 2. Of those that a mesh axis runs over, the one named last changes fastest.
Arguments:
- tokens: bfloat16 [4096, 4096], P(('mod', 'seq'), 'tp'), may hold values from -6 to 6
- modality: int32 [4096], replicated, may hold values from 0 to 1, as said below
- norm_gain: float32 [2, 4096], replicated, may hold values from 0.1 to 1.9
- input_weight: bfloat16 [2, 4096, 3, 4096], P('mod', None, None, 'tp'), may hold values from -0.09375 to 0.09375
- head_gain: float32 [2, 2, 128], replicated, may hold values from 1 to 2
- output_weight: bfloat16 [2, 4096, 4096], P('mod', 'tp'), may hold values from -0.125 to 0.125
Outputs:
- update: bfloat16 [4096, 4096], P(('mod', 'seq'), 'tp')
Inputs may be any that keep to these rules, and one draw needn't show every extreme that they name: Each value is constant over aligned spans of 64 tokens. Each token shard (the 512 tokens of one index of mod+seq) holds between 3 and 5 image spans, so at most 320 tokens of either modality. In every draw, for some index of seq both of its token shards hold 320 text tokens, and for another index of seq both hold 320 image tokens.
All inputs are finite; a program needn't handle non-finite values.
Results may differ from a plain program's by a relative error of at most 0.019.
Values may be sent and summed in bfloat16 or wider, within the bound.
No kernel may reach another device: no remote copies, remote signals or barrier semaphores. Data moves between devices by JAX's collectives and lax.ppermute only.
A program may use at most 256 MiB of HBM per device.

v0:
```python
from functools import partial
import math

import jax
import jax.numpy as jnp
from jax import lax
from jax.experimental import pallas as pl
from jax.experimental.pallas import tpu as pltpu
from jax.sharding import PartitionSpec as P

HD = 128
CAP = 320
SPAN = 64
SLOTS = CAP // SPAN
VMEM = 56 * 1024 * 1024


epsilon = 1e-05
sentinel = 1 << 30


def route_table(shard_ids, shard_index, slot_count):
    length = shard_ids.shape[0]
    order = jnp.argsort(shard_ids, stable=True)
    text_count = jnp.sum((shard_ids == 0).astype(jnp.int32))
    padded = jnp.concatenate([order, jnp.zeros((slot_count,), jnp.int32)])
    slot_index = jnp.arange(slot_count, dtype=jnp.int32)
    picked = jnp.stack(
        [padded[:slot_count], lax.dynamic_slice_in_dim(padded, text_count, slot_count)]
    )
    live = jnp.stack([slot_index < text_count, slot_index < length - text_count])
    place = shard_index * length + picked
    query_place = jnp.where(live, place, -1)
    key_place = jnp.where(live, place, sentinel)
    return (order, text_count, picked, live, query_place, key_place)


def select_rows(table, picked, live):
    return jnp.where(live[:, :, None], table[picked], jnp.zeros((), table.dtype))


def head_norm(part, gain):
    return part * lax.rsqrt(jnp.mean(part * part, axis=-1, keepdims=True) + epsilon) * gain


def general_body(tokens, modality, norm_gain, input_weight, head_gain, output_weight):
    length = tokens.shape[0]
    mod_count = lax.axis_size("mod")
    seq_count = lax.axis_size("seq")
    shards = mod_count * seq_count
    mine = lax.axis_index("mod")
    seq_index = lax.axis_index("seq")
    all_ids = modality.reshape(shards, length)
    own_index = mine * seq_count + seq_index
    own_ids = lax.dynamic_index_in_dim(all_ids, own_index, 0, keepdims=False)
    own_table = route_table(own_ids, own_index, CAP)
    order = own_table[0]
    text_count = own_table[1]
    picked = own_table[2]
    live = own_table[3]
    tables = jax.vmap(partial(route_table, slot_count=CAP))(
        all_ids, jnp.arange(shards, dtype=jnp.int32)
    )
    query_grid = tables[4].reshape(mod_count, seq_count, 2, CAP)
    own_query = lax.dynamic_index_in_dim(query_grid, seq_index, 1, keepdims=False)
    own_query = lax.dynamic_index_in_dim(own_query, mine, 1, keepdims=False).reshape(
        mod_count * CAP
    )
    key_grid = tables[5].reshape(mod_count, seq_count, 2, CAP)
    key_order = jnp.transpose(key_grid, (2, 1, 0, 3)).reshape(shards * mod_count * CAP)
    gathered = lax.all_gather(tokens, "tp", axis=1, tiled=True)
    arrived = lax.all_to_all(
        select_rows(gathered, picked, live), "mod", split_axis=0, concat_axis=0, tiled=True
    )
    rows_total = arrived.shape[0] * arrived.shape[1]
    width = arrived.shape[2]
    states = arrived.reshape(rows_total, width).astype(jnp.float32)
    gain = lax.dynamic_index_in_dim(norm_gain, mine, 0, keepdims=False)
    normed = (
        states * lax.rsqrt(jnp.mean(states * states, axis=1, keepdims=True) + epsilon) * gain
    ).astype(jnp.bfloat16)
    local_width = input_weight.shape[3]
    heads_here = local_width // HD
    projected = jnp.dot(
        normed, input_weight[0].reshape(width, 3 * local_width), preferred_element_type=jnp.float32
    )
    projected = projected.reshape(rows_total, 3, heads_here, HD)
    gains = lax.dynamic_index_in_dim(head_gain, mine, 0, keepdims=False)
    query_rows = head_norm(projected[:, 0], gains[0]).astype(jnp.bfloat16)
    key_rows = (
        head_norm(projected[:, 1], gains[1]).astype(jnp.bfloat16).reshape(rows_total, local_width)
    )
    value_rows = projected[:, 2].astype(jnp.bfloat16).reshape(rows_total, local_width)
    scale = 1.0 / math.sqrt(HD)
    key_piece = lax.all_gather(key_rows, ("mod", "seq"), axis=0, tiled=True)
    value_piece = lax.all_gather(value_rows, ("mod", "seq"), axis=0, tiled=True)
    count = key_piece.shape[0]
    scores = (
        jnp.einsum(
            "rhe,khe->hrk",
            query_rows,
            key_piece.reshape(count, heads_here, HD),
            preferred_element_type=jnp.float32,
        )
        * scale
    )
    weights = jnp.where(key_order[None, None, :] <= own_query[None, :, None], jnp.exp(scores), 0.0)
    totals = jnp.sum(weights, axis=2)
    rounded = weights.astype(jnp.bfloat16)
    weighted = jnp.einsum(
        "hrk,khe->rhe",
        rounded,
        value_piece.reshape(count, heads_here, HD),
        preferred_element_type=jnp.float32,
    )
    weighted, totals = (weighted, totals)
    totals = jnp.where(own_query[None, :] >= 0, totals, 1.0)
    attention = (
        (weighted / jnp.transpose(totals)[:, :, None])
        .astype(jnp.bfloat16)
        .reshape(rows_total, local_width)
    )
    head_terms = jnp.dot(attention, output_weight[0], preferred_element_type=jnp.float32)
    summed = lax.psum_scatter(
        head_terms.astype(jnp.bfloat16), "tp", scatter_dimension=1, tiled=True
    ).astype(jnp.float32)
    result = summed.astype(jnp.bfloat16).reshape(mod_count, CAP, summed.shape[1])
    returned = lax.all_to_all(result, "mod", split_axis=0, concat_axis=0, tiled=True)
    flat = returned.reshape(mod_count * CAP, summed.shape[1])
    inverse = jnp.zeros((length,), jnp.int32).at[order].set(jnp.arange(length, dtype=jnp.int32))
    slot = own_ids * CAP + inverse - own_ids * text_count
    return flat[slot]


def swap(size, bit):
    return [(i, i ^ bit) for i in range(size)]


def half_kernel(parts, meta, weight, *refs):
    out, held, come, gone = refs[-4:]
    half = out.shape[2]
    depth = held.shape[1]
    start = pl.multiple_of((1 - meta[0]) * half, half)
    inward, outward = [], []
    for n, part in enumerate(parts):
        for f in range(out.shape[1] // depth):
            at, deep = len(inward), pl.ds(f * depth, depth)
            source = weight.at[part, deep, pl.ds(start, half)]
            inward.append(pltpu.make_async_copy(source, held.at[at], come.at[at]))
            outward.append(pltpu.make_async_copy(held.at[at], out.at[n, deep, :], gone.at[at]))
    for copy in inward:
        copy.start()
    for first, second in zip(inward, outward):
        first.wait()
        second.start()
    for copy in outward:
        copy.wait()


def other_half(meta, after, weight, parts):
    outside = pl.BlockSpec(memory_space=pl.ANY)
    depth, half = weight.shape[1], weight.shape[2] // 2
    count = 4 * len(parts)
    return pl.pallas_call(
        partial(half_kernel, parts),
        in_specs=[pl.BlockSpec(memory_space=pltpu.SMEM)] + [outside] * (1 + len(after)),
        out_specs=outside,
        out_shape=jax.ShapeDtypeStruct((len(parts), depth, half), weight.dtype),
        scratch_shapes=[
            pltpu.VMEM((count, depth // 4, half), weight.dtype),
            pltpu.SemaphoreType.DMA((count,)),
            pltpu.SemaphoreType.DMA((count,)),
        ],
        compiler_params=pltpu.CompilerParams(vmem_limit_bytes=VMEM),
        cost_estimate=pl.CostEstimate(flops=count * 1000000000, bytes_accessed=1000, transcendentals=0),
        name="other_half",
    )(meta, weight, *after)


def project_kernel(chunk, meta, ids, block, p1, p2, p3a, p3b, q, gain, head_gain, own_w, early_w, late_w, out, rows, inverse, tiles, table, sems):
    mine, seq, tp = meta[0], meta[1], meta[2]
    width, half = tiles.shape[2:]
    features = 4 * width
    quarter = p3a.shape[0]

    def part_of(step):
        which = lax.rem(step, 3)
        return jnp.where(which == 0, 1, jnp.where(which == 1, 0, 2))

    def copies(step, act):
        which = lax.rem(step, 3)
        for f in range(4):
            deep = pl.ds(f * width, width)
            slot = lax.rem(step, 2) * 4 + f

            def move(source):
                act(pltpu.make_async_copy(source, tiles.at[lax.rem(step, 2), f], sems.at[slot]))

            @pl.when(step < 3)
            def _():
                move(own_w.at[part_of(step), deep, pl.ds(pl.multiple_of(mine * half, half), half)])

            @pl.when((step == 3) | (step == 4))
            def _():
                move(early_w.at[jnp.minimum(which, 1), deep, :])

            @pl.when(step == 5)
            def _():
                move(late_w.at[0, deep, :])

    for step in range(2):
        copies(jnp.int32(step), lambda copy: copy.start())

    counts = [jnp.int32(0), jnp.int32(0)]
    for j in range(8):
        near, at = j < 4, j % 4
        span = 4 * mine + at if near else 4 * (1 - mine) + at
        kind = ids[((chunk * 4 + seq) * 8 + span) * SPAN]
        same = (kind == mine).astype(jnp.int32)
        group = 1 - same
        slot = jnp.where(same == 1, counts[0], counts[1])
        counts = [counts[0] + same, counts[1] + group]
        table[group * 8 + slot] = span
        place = pl.ds(pl.multiple_of(slot * SPAN, SPAN), SPAN)
        total = jnp.zeros((SPAN, 1), jnp.float32)
        for k in range(4):
            if k == 0:
                value = block[pl.ds(pl.multiple_of(span * SPAN, SPAN), SPAN), :]
            elif not near:
                start = (k - 1) * 2 * quarter + at * SPAN
                value = q[start : start + SPAN, :]
            else:
                ref, base = ((p1, 0), (p2, 0), ((p3a, p3b)[at // 2], at // 2 * 2))[k - 1]
                value = ref[(at - base) * SPAN : (at - base + 1) * SPAN, :]
            value = value.astype(jnp.float32)
            total += jnp.sum(value * value, axis=1, keepdims=True)
            feature = tp ^ k
            scale = gain[pl.ds(kind, 1), pl.ds(pl.multiple_of(feature * width, width), width)]
            rows[feature, group, place, :] = (value * scale).astype(jnp.bfloat16)
        scale = lax.rsqrt(total / features + epsilon)
        inverse[group, place, :] = jnp.broadcast_to(scale, (SPAN, HD))
    table[16] = counts[0]
    table[17] = counts[1]

    @pl.loop(0, 6)
    def _(step):
        group = (step >= 3).astype(jnp.int32)
        copies(step, lambda copy: copy.wait())
        buffer = lax.rem(step, 2)
        total = None
        for f in range(4):
            term = jnp.dot(rows[f, group], tiles[buffer, f], preferred_element_type=jnp.float32)
            total = term if total is None else total + term
        @pl.when(step < 4)
        def _():
            copies(step + 2, lambda copy: copy.start())

        kind = jnp.where(group == 0, mine, 1 - mine)
        which = part_of(step)
        scale = inverse[group]
        count = table[16 + group]
        row = head_gain[kind, pl.ds(jnp.minimum(which, 1), 1), :]
        row = row * jnp.where(which == 0, math.log2(math.e) / math.sqrt(HD), 1.0)
        for h in range(4):
            piece = total[:, h * HD : (h + 1) * HD] * scale
            mean = jnp.mean(piece * piece, axis=1, keepdims=True)
            normed = piece * lax.rsqrt(mean + epsilon) * row
            value = jnp.where(which == 2, piece, normed).astype(jnp.bfloat16)
            for slot in range(SLOTS):

                @pl.when(slot < count)
                def _():
                    span = table[group * 8 + slot]
                    out[h, which, pl.ds(pl.multiple_of(span * SPAN, SPAN), SPAN), :] = value[
                        slot * SPAN : (slot + 1) * SPAN
                    ]


def project(chunk, meta, ids, pieces, gain, head_gain, own_w, early_w, late_w):
    depth, half = early_w.shape[1:]
    width = depth // 4
    whole = pl.BlockSpec(memory_space=pltpu.VMEM)
    scalars = pl.BlockSpec(memory_space=pltpu.SMEM)
    outside = pl.BlockSpec(memory_space=pl.ANY)
    shape = jax.ShapeDtypeStruct((4, 3, 8 * SPAN, HD), jnp.bfloat16)
    return pl.pallas_call(
        partial(project_kernel, chunk),
        in_specs=[scalars] * 2 + [whole] * 8 + [outside] * 3,
        out_specs=whole,
        scratch_shapes=[
            pltpu.VMEM((4, 2, CAP, width), jnp.bfloat16),
            pltpu.VMEM((2, CAP, HD), jnp.float32),
            pltpu.VMEM((2, 4, width, half), jnp.bfloat16),
            pltpu.SMEM((32,), jnp.int32),
            pltpu.SemaphoreType.DMA((8,)),
        ],
        out_shape=shape,
        compiler_params=pltpu.CompilerParams(vmem_limit_bytes=VMEM),
        cost_estimate=pl.CostEstimate(flops=20000000000, bytes_accessed=1000, transcendentals=0),
        name="project",
    )(meta, ids, *pieces, gain, head_gain, own_w, early_w, late_w)


def attend_kernel(high, meta, after, later, *refs):
    first, last = refs[0], refs[1] if high else refs[0]
    out, values = refs[-2:]
    block = last.shape[2]
    half = block // 2
    for base, pieces in ((0, first), (4, last)) if high else ((0, first),):
        for at in range(4):
            values[base + at, :, :HD] = pieces[at, 2]
            values[base + at, :, HD:] = jnp.ones((block, HD), jnp.bfloat16)
    diagonal = lax.broadcasted_iota(jnp.int32, (half, half), 0) >= lax.broadcasted_iota(
        jnp.int32, (half, half), 1
    )

    def scores(query, key):
        return lax.dot_general(query, key, (((1,), (1,)), ((), ())), preferred_element_type=jnp.float32)

    for at in range(4):
        own = 4 + at if high else at
        for side in range(2):
            query = last[at, 0, side * half : (side + 1) * half, :]
            weight = jnp.where(
                diagonal, jnp.exp2(scores(query, last[at, 1, side * half : (side + 1) * half, :])), 0.0
            ).astype(jnp.bfloat16)
            total = jnp.dot(
                weight, values[own, side * half : (side + 1) * half, :], preferred_element_type=jnp.float32
            )
            if side == 1:
                weight = jnp.exp2(scores(query, last[at, 1, :half, :])).astype(jnp.bfloat16)
                total += jnp.dot(weight, values[own, :half, :], preferred_element_type=jnp.float32)

            for j in range(own):
                key = first[j, 1] if j < 4 else last[j - 4, 1]
                weight = jnp.exp2(scores(query, key)).astype(jnp.bfloat16)
                total += jnp.dot(weight, values[j], preferred_element_type=jnp.float32)
            out[side, at] = (total[:, :HD] / total[:, HD:]).astype(jnp.bfloat16)


def attend(meta, after, later, first, last=None):
    high = last is not None
    pieces = [first, last] if high else [first]
    block = first.shape[2]
    whole = pl.BlockSpec(memory_space=pltpu.VMEM)
    count = 8 if high else 4
    return pl.pallas_call(
        partial(attend_kernel, high),
        in_specs=[pl.BlockSpec(memory_space=pltpu.SMEM)]
        + [pl.BlockSpec(memory_space=pl.ANY)] * 2
        + [whole] * len(pieces),
        out_specs=whole,
        out_shape=jax.ShapeDtypeStruct((2, 4, block // 2, HD), jnp.bfloat16),
        scratch_shapes=[
            pltpu.VMEM((count, block, 2 * HD), jnp.bfloat16),
        ],
        compiler_params=pltpu.CompilerParams(vmem_limit_bytes=VMEM),
        cost_estimate=pl.CostEstimate(flops=12000000000 if high else 6000000000, bytes_accessed=1000, transcendentals=0),
        name="attend",
    )(meta, after, later, *pieces)


ORDER = (3, 1, 2, 0)


def finish_kernel(chunk, meta, ids, after, heads, own_w, other_w, to_x, to_y, keep_a, keep_b, rows):
    step = pl.program_id(0)
    mine, seq = meta[0], meta[1]

    @pl.when(step == 0)
    def _():
        for j in range(4):
            same = ids[((chunk * 4 + seq) * 8 + 4 * mine + j) * SPAN] == mine
            for h in range(8):
                value = heads[h, j * SPAN : (j + 1) * SPAN, :]
                zero = jnp.zeros_like(value)
                rows[0, j * SPAN : (j + 1) * SPAN, h * HD : (h + 1) * HD] = jnp.where(same, value, zero)
                rows[1, j * SPAN : (j + 1) * SPAN, h * HD : (h + 1) * HD] = jnp.where(same, zero, value)

    term = jnp.dot(rows[0], own_w[...], preferred_element_type=jnp.float32)
    term += jnp.dot(rows[1], other_w[...], preferred_element_type=jnp.float32)
    term = term.astype(jnp.bfloat16)
    half = term.shape[0] // 2
    places = {
        0: ((keep_a, 0), (keep_b, 0)),
        1: ((to_x, 0), (keep_b, 1)),
        2: ((keep_a, 1), (to_y, 0)),
        3: ((to_x, 1), (to_y, 1)),
    }
    for at, k in enumerate(ORDER):

        @pl.when(step == at)
        def _():
            (a, i), (b, j) = places[k]
            a[i] = term[:half]
            b[j] = term[half:]


def finish(chunk, meta, ids, after, heads, own_w, other_w):
    depth, total = own_w.shape
    width = total // 4
    count = heads.shape[1]
    whole = pl.BlockSpec(memory_space=pltpu.VMEM)

    def column(i, meta, ids):
        k = jnp.where(i == 0, 3, jnp.where(i == 3, 0, i))
        return (0, meta[2] ^ k)

    shape = jax.ShapeDtypeStruct((2, count // 2, width), jnp.bfloat16)
    return pl.pallas_call(
        partial(finish_kernel, chunk),
        grid_spec=pltpu.PrefetchScalarGridSpec(
            num_scalar_prefetch=2,
            grid=(4,),
            in_specs=[pl.BlockSpec(memory_space=pl.ANY), whole, pl.BlockSpec((depth, width), column), pl.BlockSpec((depth, width), column)],
            out_specs=[whole] * 4,
            scratch_shapes=[pltpu.VMEM((2, count, depth), jnp.bfloat16)],
        ),
        out_shape=[shape] * 4,
        compiler_params=pltpu.CompilerParams(vmem_limit_bytes=VMEM),
        cost_estimate=pl.CostEstimate(flops=12000000000, bytes_accessed=1000, transcendentals=0),
        name="finish",
    )(meta, ids, after, heads, own_w, other_w)


def body(tokens, modality, norm_gain, input_weight, head_gain, output_weight):
    mine, seq, tp = lax.axis_index("mod"), lax.axis_index("seq"), lax.axis_index("tp")
    width = tokens.shape[1]
    half = input_weight.shape[3] // 2
    first = mine == 0
    meta = jnp.stack([mine, seq, tp]).astype(jnp.int32)

    def to_mod(value):
        return lax.ppermute(value, "mod", swap(2, 1))

    def to_x(value):
        return lax.ppermute(value, "tp", swap(4, 1))

    def to_y(value):
        return lax.ppermute(value, "tp", swap(4, 2))

    own_w = jnp.transpose(input_weight[0], (1, 0, 2))
    partner = to_mod(tokens)
    early_half = other_half(meta, [], own_w, (1, 0))
    partner, early_half = lax.optimization_barrier((partner, early_half))
    blocks = [jnp.where(first, tokens, partner), jnp.where(first, partner, tokens)]
    rows = blocks[0].shape[0] // 2
    quarter = rows // 2
    starts = [lax.dynamic_slice_in_dim(block, mine * rows, rows, axis=0) for block in blocks]
    low_x, low_y, early_w = to_x(starts[0]), to_y(starts[0]), to_mod(early_half)
    low_x, low_y, start_high = lax.optimization_barrier((low_x, low_y, starts[1]))
    late_w = to_mod(other_half(meta, [low_x, low_y], own_w, (2,)))
    high_x, high_y = to_x(start_high), to_y(start_high)
    own_out = output_weight[0]
    arrived, projected = [], []
    for chunk, pieces in enumerate(([low_x, low_y], [high_x, high_y])):
        if chunk:
            pieces[0], pieces[1], late_out, _ = lax.optimization_barrier((high_x, high_y, own_out, projected[0]))
            other_out = to_mod(late_out)
        pieces = pieces + [to_y(pieces[0][:quarter]), to_x(pieces[1][quarter:])]
        q = to_mod(jnp.concatenate(pieces))
        pieces = [blocks[chunk]] + pieces + [q]
        sent = project(chunk, meta, modality, pieces, norm_gain, head_gain, own_w, early_w, late_w)
        arrived.append(lax.all_to_all(sent, "seq", 0, 0, tiled=True))
        projected.append(sent)
    low_mixed = attend(meta, projected[1], projected[1], arrived[0])
    low_mixed, arrived[1] = lax.optimization_barrier((low_mixed, arrived[1]))
    high_mixed = attend(meta, low_mixed, other_out, *arrived)

    results = []
    for chunk, mixed in enumerate((low_mixed, high_mixed)):
        mixed = mixed.reshape((8,) + mixed.shape[2:])
        heads = lax.all_to_all(mixed, ("mod", "seq"), 0, 0, tiled=True)
        send_x, send_y, keep_a, keep_b = finish(chunk, meta, modality, results[-1] if chunk else high_mixed, heads, own_out, other_out)
        got_x, got_y = to_x(send_x).astype(jnp.float32), to_y(send_y).astype(jnp.float32)
        keep_a, keep_b = keep_a.astype(jnp.float32), keep_b.astype(jnp.float32)
        last_a = to_y((keep_a[1] + got_x[1]).astype(jnp.bfloat16)).astype(jnp.float32)
        last_b = to_x((keep_b[1] + got_y[1]).astype(jnp.bfloat16)).astype(jnp.float32)
        result = jnp.concatenate([keep_a[0] + got_x[0] + last_a, keep_b[0] + got_y[0] + last_b])
        results.append(result.astype(jnp.bfloat16))
    back = to_mod(jnp.where(first, results[1], results[0]))
    return jnp.concatenate(
        [jnp.where(first, results[0], back), jnp.where(first, back, results[1])], axis=0
    )


def solution(mesh):
    sizes = dict(mesh.shape)
    in_specs = (
        P(("mod", "seq"), "tp"),
        P(),
        P(),
        P("mod", None, None, "tp"),
        P(),
        P("mod", "tp", None),
    )
    out_specs = P(("mod", "seq"), "tp")

    def run(tokens, modality, norm_gain, input_weight, head_gain, output_weight):
        heads = input_weight.shape[3] // HD
        shard = tokens.shape[0] // (sizes["mod"] * sizes["seq"])
        small = (sizes["mod"], sizes["seq"], sizes["tp"]) == (2, 4, 4)
        fits = small and heads == 32 and shard == 8 * SPAN
        return jax.shard_map(
            body if fits else general_body,
            mesh=mesh,
            in_specs=in_specs,
            out_specs=out_specs,
            check_vma=False,
        )(tokens, modality, norm_gain, input_weight, head_gain, output_weight)

    return run
```

profile of v0, /device:TPU:0, one launch (start us, length us, event | category | flops | bytes accessed | tf_op | source)
XLA Modules:
  0.0 253.0 jit_solution(9831272450306628151)
XLA Ops:
  1.1 7.3 %other_half.2 = bf16[2,4096,512]{2,1,0:T(8,128)(2,1)} custom-call(s32[3]{0:T(128)} %pad_add_fusion.meta, bf16[3,4096,1024]{2,1,0:T(8,128)(2,1)} %bitcast.41), custom_call_target="tpu_custom_call" | custom-call | flops 8000000000 | bytes 1000 | tf_op jit(solution)/shard_map/other_half/pallas_call | solution.py:164
  8.8 3.0 %collective-permute-start.1 = (bf16[256,1024]{1,0:T(8,128)(2,1)S(1)}, bf16[256,1024]{1,0:T(8,128)(2,1)S(1)}, u32[]{:S(2)}, u32[]{:S(2)}) collective-permute-start(bf16[256,1024]{1,0:T(8,128)(2,1)S(1)} %constant_dynamic-slice_fusion.1), channel_id=1, source_target_pairs={{0,1},{1,0},{2,3},{3,2},{4,5},{5,4},{6,7},{7,6},{8,9},{9,8},{10,11... | collective-permute-start | bytes 1572872 | tf_op jit(solution)/shard_map/ppermute | solution.py:437
  11.8 1.5 collective-permute-start.2
  13.4 10.6 %collective-permute-done.1.refs_0_.p1 = bf16[256,1024]{1,0:T(8,128)(2,1)S(1)} collective-permute-done((bf16[256,1024]{1,0:T(8,128)(2,1)S(1)}, bf16[256,1024]{1,0:T(8,128)(2,1)S(1)}, u32[]{:S(2)}, u32[]{:S(2)}) %collective-permute-start.1) | collective-permute-done | bytes 524320 | tf_op jit(solution)/shard_map/ppermute | solution.py:437
  23.9 1.5 collective-permute-done.2.refs_1_.p2
  26.2 3.9 %other_half.3 = bf16[1,4096,512]{2,1,0:T(8,128)(2,1)} custom-call(s32[3]{0:T(128)} %pad_add_fusion.meta, bf16[3,4096,1024]{2,1,0:T(8,128)(2,1)} %bitcast.42, bf16[256,1024]{1,0:T(8,128)(2,1)} %copy-done, bf16[256,1024]{1,0:T(8,128)(2,1)} %copy-done.1), custom_call_target="tpu_custom_call" | custom-call | flops 4000000000 | bytes 1000 | tf_op jit(solution)/shard_map/other_half/pallas_call | solution.py:164
  30.2 1.0 slice.60
  31.2 1.0 slice.61
  32.2 1.6 collective-permute-start.5
  33.8 1.1 collective-permute-start.6
  34.8 6.1 %collective-permute-done.5.p3a = bf16[128,1024]{1,0:T(8,128)(2,1)S(1)} collective-permute-done((bf16[128,1024]{1,0:T(8,128)(2,1)S(1)}, bf16[128,1024]{1,0:T(8,128)(2,1)S(1)}, u32[]{:S(2)}, u32[]{:S(2)}) %collective-permute-start.5) | collective-permute-done | bytes 262176 | tf_op jit(solution)/shard_map/ppermute | solution.py:440
  40.9 1.2 collective-permute-done.6.p3b
  42.2 1.4 pad_maximum_fusion
  43.7 1.2 collective-permute-start.3
  45.3 1.7 collective-permute-done.7.q
  47.1 1.1 copy-done.18
  48.2 1.3 copy-done.17
  49.6 19.8 %project.2 = bf16[4,3,512,128]{3,2,1,0:T(8,128)(2,1)} custom-call(s32[3]{0:T(128)} %pad_add_fusion.meta, s32[4096]{0:T(1024)} %ids.7, bf16[512,1024]{1,0:T(8,128)(2,1)} %copy-done.3, bf16[256,1024]{1,0:T(8,128)(2,1)} %copy-done, bf16[256,1024]{1,0:T(8,128)(2,1)} %copy-done.1, bf16[128,1024]{1,0:T(8,128)(2,1)} %copy-done.13, bf16[128,1024]{1,0:T(8,128)(2,1)} %copy-done.14, ...), custom_call_target="tpu_custom_call" | custom-call | flops 20000000000 | bytes 1000 | tf_op jit(solution)/shard_map/project/pallas_call | solution.py:286
  70.3 1.2 collective-permute-start.11
  71.4 6.9 %collective-permute-done.10.p3a = bf16[128,1024]{1,0:T(8,128)(2,1)S(1)} collective-permute-done((bf16[128,1024]{1,0:T(8,128)(2,1)S(1)}, bf16[128,1024]{1,0:T(8,128)(2,1)S(1)}, u32[]{:S(2)}, u32[]{:S(2)}) %collective-permute-start.10) | collective-permute-done | bytes 262176 | tf_op jit(solution)/shard_map/ppermute | solution.py:440
  79.4 4.9 %all-to-all-start = ((bf16[4,3,512,128]{3,2,1,0:T(8,128)(2,1)}), bf16[4,3,512,128]{3,2,1,0:T(8,128)(2,1)S(1)}, u32[]{:S(2)}, u32[]{:S(2)}) async-start(bf16[4,3,512,128]{3,2,1,0:T(8,128)(2,1)} %project.2), calls=%async_computation | async-start | bytes 3145728 | tf_op jit(solution)/shard_map/all_to_all | solution.py:464
  85.1 19.8 %project.3.after.later = bf16[4,3,512,128]{3,2,1,0:T(8,128)(2,1)} custom-call(s32[3]{0:T(128)} %pad_add_fusion.meta, s32[4096]{0:T(1024)} %ids.7, bf16[512,1024]{1,0:T(8,128)(2,1)} %copy-done.2, bf16[256,1024]{1,0:T(8,128)(2,1)} %copy-done.6, bf16[256,1024]{1,0:T(8,128)(2,1)} %copy-done.7, bf16[128,1024]{1,0:T(8,128)(2,1)} %copy-done.15, ...), custom_call_target="tpu_custom_call" | custom-call | flops 20000000000 | bytes 1000 | tf_op jit(solution)/shard_map/project/pallas_call | solution.py:286
  104.9 16.5 %all-to-all-done.refs_0_ = bf16[4,3,512,128]{3,2,1,0:T(8,128)(2,1)S(1)} async-done(((bf16[4,3,512,128]{3,2,1,0:T(8,128)(2,1)}), bf16[4,3,512,128]{3,2,1,0:T(8,128)(2,1)S(1)}, u32[]{:S(2)}, u32[]{:S(2)}) %all-to-all-start) | async-done | bytes 1572896 | tf_op jit(solution)/shard_map/all_to_all | solution.py:464
  121.4 3.6 %all-to-all-start.1 = ((bf16[4,3,512,128]{3,2,1,0:T(8,128)(2,1)}), bf16[4,3,512,128]{3,2,1,0:T(8,128)(2,1)S(1)}, u32[]{:S(2)}, u32[]{:S(2)}) async-start(bf16[4,3,512,128]{3,2,1,0:T(8,128)(2,1)} %project.3.after.later), calls=%async_computation.1 | async-start | bytes 3145728 | tf_op jit(solution)/shard_map/all_to_all | solution.py:464
  124.9 5.3 %attend.2.after = bf16[2,4,256,128]{3,2,1,0:T(8,128)(2,1)} custom-call(s32[3]{0:T(128)} %pad_add_fusion.meta, bf16[4,3,512,128]{3,2,1,0:T(8,128)(2,1)} %project.3.after.later, bf16[4,3,512,128]{3,2,1,0:T(8,128)(2,1)} %project.3.after.later, bf16[4,3,512,128]{3,2,1,0:T(8,128)(2,1)} %copy-done.4), custom_call_target="tpu_custom_call" | custom-call | flops 6000000000 | bytes 1000 | tf_op jit(solution)/shard_map/attend/pallas_call | solution.py:347
  130.2 31.2 %all-to-all-done.1.refs_1_ = bf16[4,3,512,128]{3,2,1,0:T(8,128)(2,1)S(1)} async-done(((bf16[4,3,512,128]{3,2,1,0:T(8,128)(2,1)}), bf16[4,3,512,128]{3,2,1,0:T(8,128)(2,1)S(1)}, u32[]{:S(2)}, u32[]{:S(2)}) %all-to-all-start.1) | async-done | bytes 1572896 | tf_op jit(solution)/shard_map/all_to_all | solution.py:464
  161.4 3.7 %all-to-all-start.2 = ((bf16[8,256,128]{2,1,0:T(8,128)(2,1)}), bf16[8,256,128]{2,1,0:T(8,128)(2,1)S(1)}, u32[]{:S(2)}, u32[]{:S(2)}) async-start(bf16[8,256,128]{2,1,0:T(8,128)(2,1)} %bitcast.45), calls=%async_computation.2 | async-start | bytes 1048576 | tf_op jit(solution)/shard_map/all_to_all | solution.py:473
  165.1 10.1 %attend.3.after = bf16[2,4,256,128]{3,2,1,0:T(8,128)(2,1)} custom-call(s32[3]{0:T(128)} %pad_add_fusion.meta, bf16[2,4,256,128]{3,2,1,0:T(8,128)(2,1)} %attend.2.after, bf16[1024,4096]{1,0:T(8,128)(2,1)} %collective-permute-done.13.later.other_w, bf16[4,3,512,128]{3,2,1,0:T(8,128)(2,1)} %copy-done.4, bf16[4,3,512,128]{3,2,1,0:T(8,128)(2,1)} %copy-done.5), custom_call_target="tpu_custom_call" | custom-call | flops 12000000000 | bytes 1000 | tf_op jit(solution)/shard_map/attend/pallas_call | solution.py:347
  175.2 4.5 %all-to-all-done.2.heads = bf16[8,256,128]{2,1,0:T(8,128)(2,1)S(1)} async-done(((bf16[8,256,128]{2,1,0:T(8,128)(2,1)}), bf16[8,256,128]{2,1,0:T(8,128)(2,1)S(1)}, u32[]{:S(2)}, u32[]{:S(2)}) %all-to-all-start.2) | async-done | bytes 524320 | tf_op jit(solution)/shard_map/all_to_all | solution.py:473
  180.5 11.3 %finish.2 = (bf16[2,128,1024]{2,1,0:T(8,128)(2,1)}, bf16[2,128,1024]{2,1,0:T(8,128)(2,1)}, bf16[2,128,1024]{2,1,0:T(8,128)(2,1)}, bf16[2,128,1024]{2,1,0:T(8,128)(2,1)}) custom-call(s32[3]{0:T(128)} %pad_add_fusion.meta, s32[4096]{0:T(1024)} %ids.7, bf16[2,4,256,128]{3,2,1,0:T(8,128)(2,1)} %attend.3.after, bf16[8,256,128]{2,1,0:T(8,128)(2,1)} %copy-done.12, ...), custom_call_target="tpu_custom_call" | custom-call | flops 12000000000 | bytes 1000 | tf_op jit(solution)/shard_map/finish/pallas_call | solution.py:410
  191.8 1.5 collective-permute-start.16
  193.3 1.1 collective-permute-start.14
  194.4 1.1 convert_element_type.67
  195.5 3.7 %all-to-all-start.3 = ((bf16[8,256,128]{2,1,0:T(8,128)(2,1)}), bf16[8,256,128]{2,1,0:T(8,128)(2,1)S(1)}, u32[]{:S(2)}, u32[]{:S(2)}) async-start(bf16[8,256,128]{2,1,0:T(8,128)(2,1)} %bitcast.12), calls=%async_computation.3 | async-start | bytes 1048576 | tf_op jit(solution)/shard_map/all_to_all | solution.py:473
  199.3 6.8 %collective-permute-done.16 = bf16[2,128,1024]{2,1,0:T(8,128)(2,1)S(1)} collective-permute-done((bf16[2,128,1024]{2,1,0:T(8,128)(2,1)}, bf16[2,128,1024]{2,1,0:T(8,128)(2,1)S(1)}, u32[]{:S(2)}, u32[]{:S(2)}) %collective-permute-start.16) | collective-permute-done | bytes 524320 | tf_op jit(solution)/shard_map/ppermute | solution.py:440
  206.3 1.2 collective-permute-start.17
  207.7 1.6 collective-permute-start.15
  209.3 4.7 %collective-permute-done.17 = bf16[128,1024]{1,0:T(8,128)(2,1)S(1)} collective-permute-done((bf16[128,1024]{1,0:T(8,128)(2,1)S(1)}, bf16[128,1024]{1,0:T(8,128)(2,1)S(1)}, u32[]{:S(2)}, u32[]{:S(2)}) %collective-permute-start.17) | collective-permute-done | bytes 262176 | tf_op jit(solution)/shard_map/ppermute | solution.py:437
  214.1 1.1 collective-permute-done.15
  217.0 11.3 %finish.3 = (bf16[2,128,1024]{2,1,0:T(8,128)(2,1)}, bf16[2,128,1024]{2,1,0:T(8,128)(2,1)}, bf16[2,128,1024]{2,1,0:T(8,128)(2,1)}, bf16[2,128,1024]{2,1,0:T(8,128)(2,1)}) custom-call(s32[3]{0:T(128)} %pad_add_fusion.meta, s32[4096]{0:T(1024)} %ids.7, bf16[256,1024]{1,0:T(8,128)(2,1)} %pad_maximum_fusion.3.after, bf16[8,256,128]{2,1,0:T(8,128)(2,1)} %copy-done.11, ...), custom_call_target="tpu_custom_call" | custom-call | flops 12000000000 | bytes 1000 | tf_op jit(solution)/shard_map/finish/pallas_call | solution.py:410
  228.2 1.5 collective-permute-start.20
  230.7 1.1 convert_element_type.77
  231.8 8.7 %collective-permute-done.20 = bf16[2,128,1024]{2,1,0:T(8,128)(2,1)S(1)} collective-permute-done((bf16[2,128,1024]{2,1,0:T(8,128)(2,1)}, bf16[2,128,1024]{2,1,0:T(8,128)(2,1)S(1)}, u32[]{:S(2)}, u32[]{:S(2)}) %collective-permute-start.20) | collective-permute-done | bytes 524320 | tf_op jit(solution)/shard_map/ppermute | solution.py:440
  240.7 1.0 collective-permute-start.21
  243.6 3.8 %collective-permute-done.21 = bf16[128,1024]{1,0:T(8,128)(2,1)S(1)} collective-permute-done((bf16[128,1024]{1,0:T(8,128)(2,1)S(1)}, bf16[128,1024]{1,0:T(8,128)(2,1)S(1)}, u32[]{:S(2)}, u32[]{:S(2)}) %collective-permute-start.21) | collective-permute-done | bytes 262176 | tf_op jit(solution)/shard_map/ppermute | solution.py:437
  247.5 1.9 collective-permute-done.19
  249.7 1.9 collective-permute-done.22
  251.9 1.0 pad_maximum_fusion.2
  (82 shorter events, 12.4 us)
Async XLA Ops:
  0.0 8.4 %collective-permute-start = (bf16[512,1024]{1,0:T(8,128)(2,1)}, bf16[512,1024]{1,0:T(8,128)(2,1)S(1)}, u32[]{:S(2)}, u32[]{:S(2)}) collective-permute-start(bf16[512,1024]{1,0:T(8,128)(2,1)} %param.6), channel_id=1, source_target_pairs={{0,16},{16,0},{1,17},{17,1},{2,18},{18,2},{3,19},{19,3},{4,20},{20... | collective-permute-start | bytes 3145736 | tf_op jit(solution)/shard_map/ppermute | solution.py:434
  1.1 7.5 %copy-start.8 = (bf16[512,1024]{1,0:T(8,128)(2,1)S(1)}, bf16[512,1024]{1,0:T(8,128)(2,1)}, u32[]{:S(2)}) copy-start(bf16[512,1024]{1,0:T(8,128)(2,1)} %param.6) | copy-start | bytes 3145732
  8.5 38.6 %collective-permute-start.8 = (bf16[2,4096,512]{2,1,0:T(8,128)(2,1)}, bf16[2,4096,512]{2,1,0:T(8,128)(2,1)}, u32[]{:S(2)}, u32[]{:S(2)}) collective-permute-start(bf16[2,4096,512]{2,1,0:T(8,128)(2,1)} %other_half.2), channel_id=1, source_target_pairs={{0,16},{16,0},{1,17},{17,1},{2,18},{18,2},{3,19},{19,3},{4,20},{20... | collective-permute-start | bytes 25165832 | tf_op jit(solution)/shard_map/ppermute | solution.py:434
  8.7 21.4 %copy-start.2 = (bf16[512,1024]{1,0:T(8,128)(2,1)}, bf16[512,1024]{1,0:T(8,128)(2,1)S(1)}, u32[]{:S(2)}) copy-start(bf16[512,1024]{1,0:T(8,128)(2,1)S(1)} %get-tuple-element.42.block) | copy-start | bytes 3145732
  8.7 21.4 %copy-start.3 = (bf16[512,1024]{1,0:T(8,128)(2,1)}, bf16[512,1024]{1,0:T(8,128)(2,1)S(1)}, u32[]{:S(2)}) copy-start(bf16[512,1024]{1,0:T(8,128)(2,1)S(1)} %get-tuple-element.41.block) | copy-start | bytes 3145732
  8.8 15.1 %collective-permute-start.1 = (bf16[256,1024]{1,0:T(8,128)(2,1)S(1)}, bf16[256,1024]{1,0:T(8,128)(2,1)S(1)}, u32[]{:S(2)}, u32[]{:S(2)}) collective-permute-start(bf16[256,1024]{1,0:T(8,128)(2,1)S(1)} %constant_dynamic-slice_fusion.1), channel_id=1, source_target_pairs={{0,1},{1,0},{2,3},{3,2},{4,5},{5,4},{6,7},{7,6},{8,9},{9,8},{10,11... | collective-permute-start | bytes 1572872 | tf_op jit(solution)/shard_map/ppermute | solution.py:437
  11.8 13.6 %collective-permute-start.2 = (bf16[256,1024]{1,0:T(8,128)(2,1)S(1)}, bf16[256,1024]{1,0:T(8,128)(2,1)S(1)}, u32[]{:S(2)}, u32[]{:S(2)}) collective-permute-start(bf16[256,1024]{1,0:T(8,128)(2,1)S(1)} %constant_dynamic-slice_fusion.1), channel_id=1, source_target_pairs={{0,2},{1,3},{2,0},{3,1},{4,6},{5,7},{6,4},{7,5},{8,10},{9,11},{10,... | collective-permute-start | bytes 1572872 | tf_op jit(solution)/shard_map/ppermute | solution.py:440
  23.9 1.5 copy-start
  25.4 0.8 copy-start.1
  30.1 16.9 %collective-permute-start.9 = (bf16[1,4096,512]{2,1,0:T(8,128)(2,1)}, bf16[1,4096,512]{2,1,0:T(8,128)(2,1)S(1)}, u32[]{:S(2)}, u32[]{:S(2)}) collective-permute-start(bf16[1,4096,512]{2,1,0:T(8,128)(2,1)} %other_half.3), channel_id=1, source_target_pairs={{0,16},{16,0},{1,17},{17,1},{2,18},{18,2},{3,19},{19,3},{4,20},{20... | collective-permute-start | bytes 12582920 | tf_op jit(solution)/shard_map/ppermute | solution.py:434
  32.2 8.8 %collective-permute-start.5 = (bf16[128,1024]{1,0:T(8,128)(2,1)S(1)}, bf16[128,1024]{1,0:T(8,128)(2,1)S(1)}, u32[]{:S(2)}, u32[]{:S(2)}) collective-permute-start(bf16[128,1024]{1,0:T(8,128)(2,1)S(1)} %slice.60), channel_id=1, source_target_pairs={{0,2},{1,3},{2,0},{3,1},{4,6},{5,7},{6,4},{7,5},{8,10},{9,11},{10,... | collective-permute-start | bytes 786440 | tf_op jit(solution)/shard_map/ppermute | solution.py:440
  33.8 8.4 %collective-permute-start.6 = (bf16[128,1024]{1,0:T(8,128)(2,1)S(1)}, bf16[128,1024]{1,0:T(8,128)(2,1)S(1)}, u32[]{:S(2)}, u32[]{:S(2)}) collective-permute-start(bf16[128,1024]{1,0:T(8,128)(2,1)S(1)} %slice.61), channel_id=1, source_target_pairs={{0,1},{1,0},{2,3},{3,2},{4,5},{5,4},{6,7},{7,6},{8,9},{9,8},{10,11... | collective-permute-start | bytes 786440 | tf_op jit(solution)/shard_map/ppermute | solution.py:437
  40.9 6.2 %copy-start.13 = (bf16[128,1024]{1,0:T(8,128)(2,1)}, bf16[128,1024]{1,0:T(8,128)(2,1)S(1)}, u32[]{:S(2)}) copy-start(bf16[128,1024]{1,0:T(8,128)(2,1)S(1)} %collective-permute-done.5.p3a) | copy-start | bytes 786436
  42.2 4.9 %copy-start.14 = (bf16[128,1024]{1,0:T(8,128)(2,1)}, bf16[128,1024]{1,0:T(8,128)(2,1)S(1)}, u32[]{:S(2)}) copy-start(bf16[128,1024]{1,0:T(8,128)(2,1)S(1)} %collective-permute-done.6.p3b) | copy-start | bytes 786436
  43.6 3.5 %collective-permute-start.7 = (bf16[768,1024]{1,0:T(8,128)(2,1)S(1)}, bf16[768,1024]{1,0:T(8,128)(2,1)S(1)}, u32[]{:S(2)}, u32[]{:S(2)}) collective-permute-start(bf16[768,1024]{1,0:T(8,128)(2,1)S(1)} %pad_maximum_fusion), channel_id=1, source_target_pairs={{0,16},{16,0},{1,17},{17,1},{2,18},{18,2},{3,19},{19,3},{4,20},{20... | collective-permute-start | bytes 4718600 | tf_op jit(solution)/shard_map/ppermute | solution.py:434
  43.7 25.7 %collective-permute-start.3 = (bf16[256,1024]{1,0:T(8,128)(2,1)S(1)}, bf16[256,1024]{1,0:T(8,128)(2,1)S(1)}, u32[]{:S(2)}, u32[]{:S(2)}) collective-permute-start(bf16[256,1024]{1,0:T(8,128)(2,1)S(1)} %constant_dynamic-slice_fusion), channel_id=1, source_target_pairs={{0,1},{1,0},{2,3},{3,2},{4,5},{5,4},{6,7},{7,6},{8,9},{9,8},{10,11... | collective-permute-start | bytes 1572872 | tf_op jit(solution)/shard_map/ppermute | solution.py:437
  44.8 24.6 %collective-permute-start.4 = (bf16[256,1024]{1,0:T(8,128)(2,1)S(1)}, bf16[256,1024]{1,0:T(8,128)(2,1)S(1)}, u32[]{:S(2)}, u32[]{:S(2)}) collective-permute-start(bf16[256,1024]{1,0:T(8,128)(2,1)S(1)} %constant_dynamic-slice_fusion), channel_id=1, source_target_pairs={{0,2},{1,3},{2,0},{3,1},{4,6},{5,7},{6,4},{7,5},{8,10},{9,11},{10,... | collective-permute-start | bytes 1572872 | tf_op jit(solution)/shard_map/ppermute | solution.py:440
  47.1 1.1 copy-start.18
  47.1 2.5 copy-start.17
  69.4 9.2 %copy-start.6 = (bf16[256,1024]{1,0:T(8,128)(2,1)}, bf16[256,1024]{1,0:T(8,128)(2,1)S(1)}, u32[]{:S(2)}) copy-start(bf16[256,1024]{1,0:T(8,128)(2,1)S(1)} %collective-permute-done.3.p1) | copy-start | bytes 1572868
  69.4 9.3 %copy-start.7 = (bf16[256,1024]{1,0:T(8,128)(2,1)}, bf16[256,1024]{1,0:T(8,128)(2,1)S(1)}, u32[]{:S(2)}) copy-start(bf16[256,1024]{1,0:T(8,128)(2,1)S(1)} %collective-permute-done.4.p2) | copy-start | bytes 1572868
  69.5 95.6 %collective-permute-start.13 = (bf16[1024,4096]{1,0:T(8,128)(2,1)}, bf16[1024,4096]{1,0:T(8,128)(2,1)}, u32[]{:S(2)}, u32[]{:S(2)}) collective-permute-start(bf16[1024,4096]{1,0:T(8,128)(2,1)} %bitcast.46), channel_id=1, source_target_pairs={{0,16},{16,0},{1,17},{17,1},{2,18},{18,2},{3,19},{19,3},{4,20},{20... | collective-permute-start | bytes 25165832 | tf_op jit(solution)/shard_map/ppermute | solution.py:434
  69.7 8.7 %collective-permute-start.10 = (bf16[128,1024]{1,0:T(8,128)(2,1)S(1)}, bf16[128,1024]{1,0:T(8,128)(2,1)S(1)}, u32[]{:S(2)}, u32[]{:S(2)}) collective-permute-start(bf16[128,1024]{1,0:T(8,128)(2,1)S(1)} %slice.62), channel_id=1, source_target_pairs={{0,2},{1,3},{2,0},{3,1},{4,6},{5,7},{6,4},{7,5},{8,10},{9,11},{10,... | collective-permute-start | bytes 786440 | tf_op jit(solution)/shard_map/ppermute | solution.py:440
  70.3 8.4 %collective-permute-start.11 = (bf16[128,1024]{1,0:T(8,128)(2,1)S(1)}, bf16[128,1024]{1,0:T(8,128)(2,1)S(1)}, u32[]{:S(2)}, u32[]{:S(2)}) collective-permute-start(bf16[128,1024]{1,0:T(8,128)(2,1)S(1)} %slice.63), channel_id=1, source_target_pairs={{0,1},{1,0},{2,3},{3,2},{4,5},{5,4},{6,7},{7,6},{8,9},{9,8},{10,11... | collective-permute-start | bytes 786440 | tf_op jit(solution)/shard_map/ppermute | solution.py:437
  78.3 1.0 copy-start.15
  78.6 0.7 copy-start.16
  78.8 6.3 %collective-permute-start.12 = (bf16[768,1024]{1,0:T(8,128)(2,1)S(1)}, bf16[768,1024]{1,0:T(8,128)(2,1)}, u32[]{:S(2)}, u32[]{:S(2)}) collective-permute-start(bf16[768,1024]{1,0:T(8,128)(2,1)S(1)} %pad_maximum_fusion.1), channel_id=1, source_target_pairs={{0,16},{16,0},{1,17},{17,1},{2,18},{18,2},{3,19},{19,3},{4,20},{20... | collective-permute-start | bytes 4718600 | tf_op jit(solution)/shard_map/ppermute | solution.py:434
  79.4 42.0 %all-to-all-start = ((bf16[4,3,512,128]{3,2,1,0:T(8,128)(2,1)}), bf16[4,3,512,128]{3,2,1,0:T(8,128)(2,1)S(1)}, u32[]{:S(2)}, u32[]{:S(2)}) async-start(bf16[4,3,512,128]{3,2,1,0:T(8,128)(2,1)} %project.2), calls=%async_computation | async-start | bytes 3145728 | tf_op jit(solution)/shard_map/all_to_all | solution.py:464
  121.4 3.6 %copy-start.4 = (bf16[4,3,512,128]{3,2,1,0:T(8,128)(2,1)}, bf16[4,3,512,128]{3,2,1,0:T(8,128)(2,1)S(1)}, u32[]{:S(2)}) copy-start(bf16[4,3,512,128]{3,2,1,0:T(8,128)(2,1)S(1)} %all-to-all-done.refs_0_) | copy-start | bytes 4718596
  121.4 40.0 %all-to-all-start.1 = ((bf16[4,3,512,128]{3,2,1,0:T(8,128)(2,1)}), bf16[4,3,512,128]{3,2,1,0:T(8,128)(2,1)S(1)}, u32[]{:S(2)}, u32[]{:S(2)}) async-start(bf16[4,3,512,128]{3,2,1,0:T(8,128)(2,1)} %project.3.after.later), calls=%async_computation.1 | async-start | bytes 3145728 | tf_op jit(solution)/shard_map/all_to_all | solution.py:464
  161.4 3.7 %copy-start.5 = (bf16[4,3,512,128]{3,2,1,0:T(8,128)(2,1)}, bf16[4,3,512,128]{3,2,1,0:T(8,128)(2,1)S(1)}, u32[]{:S(2)}) copy-start(bf16[4,3,512,128]{3,2,1,0:T(8,128)(2,1)S(1)} %all-to-all-done.1.refs_1_) | copy-start | bytes 4718596
  161.4 18.3 %all-to-all-start.2 = ((bf16[8,256,128]{2,1,0:T(8,128)(2,1)}), bf16[8,256,128]{2,1,0:T(8,128)(2,1)S(1)}, u32[]{:S(2)}, u32[]{:S(2)}) async-start(bf16[8,256,128]{2,1,0:T(8,128)(2,1)} %bitcast.45), calls=%async_computation.2 | async-start | bytes 1048576 | tf_op jit(solution)/shard_map/all_to_all | solution.py:473
  179.7 0.8 copy-start.12
  191.8 15.7 %copy-start.9 = (bf16[2,128,1024]{2,1,0:T(8,128)(2,1)S(1)}, bf16[2,128,1024]{2,1,0:T(8,128)(2,1)}, u32[]{:S(2)}) copy-start(bf16[2,128,1024]{2,1,0:T(8,128)(2,1)} %get-tuple-element.33) | copy-start | bytes 1572868
  191.8 14.3 %collective-permute-start.16 = (bf16[2,128,1024]{2,1,0:T(8,128)(2,1)}, bf16[2,128,1024]{2,1,0:T(8,128)(2,1)S(1)}, u32[]{:S(2)}, u32[]{:S(2)}) collective-permute-start(bf16[2,128,1024]{2,1,0:T(8,128)(2,1)} %get-tuple-element.36), channel_id=1, source_target_pairs={{0,2},{1,3},{2,0},{3,1},{4,6},{5,7},{6,4},{7,5},{8,10},{9,11},{10,... | collective-permute-start | bytes 1572872 | tf_op jit(solution)/shard_map/ppermute | solution.py:440
  193.3 14.3 %collective-permute-start.14 = (bf16[2,128,1024]{2,1,0:T(8,128)(2,1)}, bf16[2,128,1024]{2,1,0:T(8,128)(2,1)S(1)}, u32[]{:S(2)}, u32[]{:S(2)}) collective-permute-start(bf16[2,128,1024]{2,1,0:T(8,128)(2,1)} %get-tuple-element.34), channel_id=1, source_target_pairs={{0,1},{1,0},{2,3},{3,2},{4,5},{5,4},{6,7},{7,6},{8,9},{9,8},{10,11... | collective-permute-start | bytes 1572872 | tf_op jit(solution)/shard_map/ppermute | solution.py:437
  195.5 20.6 %all-to-all-start.3 = ((bf16[8,256,128]{2,1,0:T(8,128)(2,1)}), bf16[8,256,128]{2,1,0:T(8,128)(2,1)S(1)}, u32[]{:S(2)}, u32[]{:S(2)}) async-start(bf16[8,256,128]{2,1,0:T(8,128)(2,1)} %bitcast.12), calls=%async_computation.3 | async-start | bytes 1048576 | tf_op jit(solution)/shard_map/all_to_all | solution.py:473
  206.3 7.8 %collective-permute-start.17 = (bf16[128,1024]{1,0:T(8,128)(2,1)S(1)}, bf16[128,1024]{1,0:T(8,128)(2,1)S(1)}, u32[]{:S(2)}, u32[]{:S(2)}) collective-permute-start(bf16[128,1024]{1,0:T(8,128)(2,1)S(1)} %fusion.17), channel_id=1, source_target_pairs={{0,1},{1,0},{2,3},{3,2},{4,5},{5,4},{6,7},{7,6},{8,9},{9,8},{10,11... | collective-permute-start | bytes 786440 | tf_op jit(solution)/shard_map/ppermute | solution.py:437
  207.7 7.5 %collective-permute-start.15 = (bf16[128,1024]{1,0:T(8,128)(2,1)S(1)}, bf16[128,1024]{1,0:T(8,128)(2,1)S(1)}, u32[]{:S(2)}, u32[]{:S(2)}) collective-permute-start(bf16[128,1024]{1,0:T(8,128)(2,1)S(1)} %fusion.16), channel_id=1, source_target_pairs={{0,2},{1,3},{2,0},{3,1},{4,6},{5,7},{6,4},{7,5},{8,10},{9,11},{10,... | collective-permute-start | bytes 786440 | tf_op jit(solution)/shard_map/ppermute | solution.py:440
  216.1 0.8 copy-start.11
  228.2 13.5 %copy-start.10 = (bf16[2,128,1024]{2,1,0:T(8,128)(2,1)S(1)}, bf16[2,128,1024]{2,1,0:T(8,128)(2,1)}, u32[]{:S(2)}) copy-start(bf16[2,128,1024]{2,1,0:T(8,128)(2,1)} %get-tuple-element.37) | copy-start | bytes 1572868
  228.2 12.3 %collective-permute-start.20 = (bf16[2,128,1024]{2,1,0:T(8,128)(2,1)}, bf16[2,128,1024]{2,1,0:T(8,128)(2,1)S(1)}, u32[]{:S(2)}, u32[]{:S(2)}) collective-permute-start(bf16[2,128,1024]{2,1,0:T(8,128)(2,1)} %get-tuple-element.40), channel_id=1, source_target_pairs={{0,2},{1,3},{2,0},{3,1},{4,6},{5,7},{6,4},{7,5},{8,10},{9,11},{10,... | collective-permute-start | bytes 1572872 | tf_op jit(solution)/shard_map/ppermute | solution.py:440
  229.7 13.0 %collective-permute-start.18 = (bf16[2,128,1024]{2,1,0:T(8,128)(2,1)}, bf16[2,128,1024]{2,1,0:T(8,128)(2,1)S(1)}, u32[]{:S(2)}, u32[]{:S(2)}) collective-permute-start(bf16[2,128,1024]{2,1,0:T(8,128)(2,1)} %get-tuple-element.38), channel_id=1, source_target_pairs={{0,1},{1,0},{2,3},{3,2},{4,5},{5,4},{6,7},{7,6},{8,9},{9,8},{10,11... | collective-permute-start | bytes 1572872 | tf_op jit(solution)/shard_map/ppermute | solution.py:437
  240.7 6.7 %collective-permute-start.21 = (bf16[128,1024]{1,0:T(8,128)(2,1)S(1)}, bf16[128,1024]{1,0:T(8,128)(2,1)S(1)}, u32[]{:S(2)}, u32[]{:S(2)}) collective-permute-start(bf16[128,1024]{1,0:T(8,128)(2,1)S(1)} %fusion.19), channel_id=1, source_target_pairs={{0,1},{1,0},{2,3},{3,2},{4,5},{5,4},{6,7},{7,6},{8,9},{9,8},{10,11... | collective-permute-start | bytes 786440 | tf_op jit(solution)/shard_map/ppermute | solution.py:437
  242.9 6.4 %collective-permute-start.19 = (bf16[128,1024]{1,0:T(8,128)(2,1)S(1)}, bf16[128,1024]{1,0:T(8,128)(2,1)S(1)}, u32[]{:S(2)}, u32[]{:S(2)}) collective-permute-start(bf16[128,1024]{1,0:T(8,128)(2,1)S(1)} %fusion.18), channel_id=1, source_target_pairs={{0,2},{1,3},{2,0},{3,1},{4,6},{5,7},{6,4},{7,5},{8,10},{9,11},{10,... | collective-permute-start | bytes 786440 | tf_op jit(solution)/shard_map/ppermute | solution.py:440
  249.7 2.0 collective-permute-start.22
where the time goes:
time: 254 us; the launch traced here: 253 us
  waiting for transfers between devices  111 us (44%)
  Pallas kernels  88.8 us (35%)
  starting transfers between devices  37 us (15%)
  other arithmetic  8.18 us (3%)
  local copies, waits for them, and re-layouts  7.45 us (3%)
    all_to_all x2, waiting for transfers between devices, body(): arrived.append(lax.all_to_all(sent, 'seq', 0, 0, tiled=True))  47.7 us
    pallas_call x2, Pallas kernels, project(): pl.pallas_call(partial(project_kernel, chunk), in_specs=[scalars] * 2 + [...  39.6 us
    ppermute x8, waiting for transfers between devices, to_y(): return lax.ppermute(value, 'tp', swap(4, 2))  33 us
    pallas_call x2, Pallas kernels, finish(): pl.pallas_call(partial(finish_kernel, chunk), grid_spec=pltpu.PrefetchSca...  22.5 us
    ppermute x8, waiting for transfers between devices, to_x(): return lax.ppermute(value, 'tp', swap(4, 1))  21.5 us
    pallas_call x2, Pallas kernels, attend(): pl.pallas_call(partial(attend_kernel, high), in_specs=[pl.BlockSpec(memor...  15.4 us
    pallas_call x2, Pallas kernels, other_half(): pl.pallas_call(partial(half_kernel, parts), in_specs=[pl.BlockSpec(memory...  11.3 us
    ppermute x8, starting transfers between devices, to_x(): return lax.ppermute(value, 'tp', swap(4, 1))  10.6 us
  transfers between devices with their start and end apart: 27, of which 19 were waited for; matrix products, arithmetic and copies ran while one was open for 3% of the time, Pallas kernels for 26%

commit v1 on v0

--- a/solution.py
+++ b/solution.py
@@ -12,7 +12,7 @@
 CAP = 320
 SPAN = 64
 SLOTS = CAP // SPAN
-VMEM = 56 * 1024 * 1024
+VMEM = 40 * 1024 * 1024
 
 
 epsilon = 1e-05
@@ -177,11 +177,19 @@
     )(meta, weight, *after)
 
 
-def project_kernel(chunk, meta, ids, block, p1, p2, p3a, p3b, q, gain, head_gain, own_w, early_w, late_w, out, rows, inverse, tiles, table, sems):
+def project_kernel(chunk, meta, ids, block, p1, p2, p3a, p3b, q, gain, head_gain, own_w, early_w, query_w, value_w, out, rows, inverse, tiles, held, table, sems):
     mine, seq, tp = meta[0], meta[1], meta[2]
     width, half = tiles.shape[2:]
     features = 4 * width
-    quarter = p3a.shape[0]
+    count = block.shape[0]
+    incoming, place = [], 0
+    for n, piece in enumerate((block, p1, p2, p3a, p3b, q)):
+        incoming.append(
+            pltpu.make_async_copy(piece, held.at[pl.ds(place, piece.shape[0]), :], sems.at[8 + n])
+        )
+        place += piece.shape[0]
+    for copy in incoming:
+        copy.start()
 
     def part_of(step):
         which = lax.rem(step, 3)
@@ -200,17 +208,23 @@
             def _():
                 move(own_w.at[part_of(step), deep, pl.ds(pl.multiple_of(mine * half, half), half)])
 
-            @pl.when((step == 3) | (step == 4))
+            @pl.when(step == 3)
             def _():
-                move(early_w.at[jnp.minimum(which, 1), deep, :])
+                move(early_w.at[0, deep, :])
+
+            @pl.when(step == 4)
+            def _():
+                move(query_w.at[0, deep, :])
 
             @pl.when(step == 5)
             def _():
-                move(late_w.at[0, deep, :])
+                move(value_w.at[0, deep, :])
 
     for step in range(2):
         copies(jnp.int32(step), lambda copy: copy.start())
 
+    for copy in incoming:
+        copy.wait()
     counts = [jnp.int32(0), jnp.int32(0)]
     for j in range(8):
         near, at = j < 4, j % 4
@@ -225,13 +239,10 @@
         total = jnp.zeros((SPAN, 1), jnp.float32)
         for k in range(4):
             if k == 0:
-                value = block[pl.ds(pl.multiple_of(span * SPAN, SPAN), SPAN), :]
-            elif not near:
-                start = (k - 1) * 2 * quarter + at * SPAN
-                value = q[start : start + SPAN, :]
+                value = held[pl.ds(pl.multiple_of(span * SPAN, SPAN), SPAN), :]
             else:
-                ref, base = ((p1, 0), (p2, 0), ((p3a, p3b)[at // 2], at // 2 * 2))[k - 1]
-                value = ref[(at - base) * SPAN : (at - base + 1) * SPAN, :]
+                start = count + (0 if near else 3 * count // 2) + (k - 1) * count // 2 + at * SPAN
+                value = held[start : start + SPAN, :]
             value = value.astype(jnp.float32)
             total += jnp.sum(value * value, axis=1, keepdims=True)
             feature = tp ^ k
@@ -285,25 +296,27 @@
     shape = jax.ShapeDtypeStruct((4, 3, 8 * SPAN, HD), jnp.bfloat16)
     return pl.pallas_call(
         partial(project_kernel, chunk),
-        in_specs=[scalars] * 2 + [whole] * 8 + [outside] * 3,
+        in_specs=[scalars] * 2 + [outside] * 6 + [whole] * 2 + [outside] * 4,
         out_specs=whole,
         scratch_shapes=[
             pltpu.VMEM((4, 2, CAP, width), jnp.bfloat16),
             pltpu.VMEM((2, CAP, HD), jnp.float32),
             pltpu.VMEM((2, 4, width, half), jnp.bfloat16),
+            pltpu.VMEM((4 * 8 * SPAN, width), jnp.bfloat16),
             pltpu.SMEM((32,), jnp.int32),
-            pltpu.SemaphoreType.DMA((8,)),
+            pltpu.SemaphoreType.DMA((14,)),
         ],
         out_shape=shape,
         compiler_params=pltpu.CompilerParams(vmem_limit_bytes=VMEM),
-        cost_estimate=pl.CostEstimate(flops=20000000000, bytes_accessed=1000, transcendentals=0),
+        cost_estimate=pl.CostEstimate(flops=1000, bytes_accessed=1000, transcendentals=0),
         name="project",
-    )(meta, ids, *pieces, gain, head_gain, own_w, early_w, late_w)
+    )(meta, ids, *pieces, gain, head_gain, own_w, early_w, *late_w)
 
 
 def attend_kernel(high, meta, after, later, *refs):
     first, last = refs[0], refs[1] if high else refs[0]
-    out, values = refs[-2:]
+    outs, (mixed, values) = refs[-6:-2], refs[-2:]
+    seq = meta[1]
     block = last.shape[2]
     half = block // 2
     for base, pieces in ((0, first), (4, last)) if high else ((0, first),):
@@ -335,7 +348,9 @@
                 key = first[j, 1] if j < 4 else last[j - 4, 1]
                 weight = jnp.exp2(scores(query, key)).astype(jnp.bfloat16)
                 total += jnp.dot(weight, values[j], preferred_element_type=jnp.float32)
-            out[side, at] = (total[:, :HD] / total[:, HD:]).astype(jnp.bfloat16)
+            mixed[at, side * half : (side + 1) * half, :] = (total[:, :HD] / total[:, HD:]).astype(jnp.bfloat16)
+    for k, out in enumerate(outs):
+        out[...] = mixed[seq ^ k]
 
 
 def attend(meta, after, later, first, last=None):
@@ -349,9 +364,10 @@
         in_specs=[pl.BlockSpec(memory_space=pltpu.SMEM)]
         + [pl.BlockSpec(memory_space=pl.ANY)] * 2
         + [whole] * len(pieces),
-        out_specs=whole,
-        out_shape=jax.ShapeDtypeStruct((2, 4, block // 2, HD), jnp.bfloat16),
+        out_specs=[whole] * 4,
+        out_shape=[jax.ShapeDtypeStruct((block, HD), jnp.bfloat16)] * 4,
         scratch_shapes=[
+            pltpu.VMEM((4, block, HD), jnp.bfloat16),
             pltpu.VMEM((count, block, 2 * HD), jnp.bfloat16),
         ],
         compiler_params=pltpu.CompilerParams(vmem_limit_bytes=VMEM),
@@ -363,7 +379,8 @@
 ORDER = (3, 1, 2, 0)
 
 
-def finish_kernel(chunk, meta, ids, after, heads, own_w, other_w, to_x, to_y, keep_a, keep_b, rows):
+def finish_kernel(chunk, meta, ids, after, *refs):
+    heads, (partner, own_w, other_w, to_x, to_y, keep_a, keep_b, rows) = refs[:4], refs[4:]
     step = pl.program_id(0)
     mine, seq = meta[0], meta[1]
 
@@ -371,11 +388,14 @@
     def _():
         for j in range(4):
             same = ids[((chunk * 4 + seq) * 8 + 4 * mine + j) * SPAN] == mine
-            for h in range(8):
-                value = heads[h, j * SPAN : (j + 1) * SPAN, :]
+            at = pl.multiple_of((4 * mine + j) * SPAN, SPAN)
+            for k in range(8):
+                value = heads[k][pl.ds(at, SPAN), :] if k < 4 else partner[k - 4, j * SPAN : (j + 1) * SPAN, :]
                 zero = jnp.zeros_like(value)
-                rows[0, j * SPAN : (j + 1) * SPAN, h * HD : (h + 1) * HD] = jnp.where(same, value, zero)
-                rows[1, j * SPAN : (j + 1) * SPAN, h * HD : (h + 1) * HD] = jnp.where(same, zero, value)
+                head = (mine ^ (k // 4)) * 4 + (seq ^ (k % 4))
+                lanes = pl.ds(pl.multiple_of(head * HD, HD), HD)
+                rows[0, j * SPAN : (j + 1) * SPAN, lanes] = jnp.where(same, value, zero)
+                rows[1, j * SPAN : (j + 1) * SPAN, lanes] = jnp.where(same, zero, value)
 
     term = jnp.dot(rows[0], own_w[...], preferred_element_type=jnp.float32)
     term += jnp.dot(rows[1], other_w[...], preferred_element_type=jnp.float32)
@@ -399,7 +419,7 @@
 def finish(chunk, meta, ids, after, heads, own_w, other_w):
     depth, total = own_w.shape
     width = total // 4
-    count = heads.shape[1]
+    count = heads[-1].shape[1]
     whole = pl.BlockSpec(memory_space=pltpu.VMEM)
 
     def column(i, meta, ids):
@@ -412,7 +432,9 @@
         grid_spec=pltpu.PrefetchScalarGridSpec(
             num_scalar_prefetch=2,
             grid=(4,),
-            in_specs=[pl.BlockSpec(memory_space=pl.ANY), whole, pl.BlockSpec((depth, width), column), pl.BlockSpec((depth, width), column)],
+            in_specs=[pl.BlockSpec(memory_space=pl.ANY)]
+            + [whole] * 5
+            + [pl.BlockSpec((depth, width), column), pl.BlockSpec((depth, width), column)],
             out_specs=[whole] * 4,
             scratch_shapes=[pltpu.VMEM((2, count, depth), jnp.bfloat16)],
         ),
@@ -420,7 +442,7 @@
         compiler_params=pltpu.CompilerParams(vmem_limit_bytes=VMEM),
         cost_estimate=pl.CostEstimate(flops=12000000000, bytes_accessed=1000, transcendentals=0),
         name="finish",
-    )(meta, ids, after, heads, own_w, other_w)
+    )(meta, ids, after, *heads, own_w, other_w)
 
 
 def body(tokens, modality, norm_gain, input_weight, head_gain, output_weight):
@@ -441,7 +463,7 @@
 
     own_w = jnp.transpose(input_weight[0], (1, 0, 2))
     partner = to_mod(tokens)
-    early_half = other_half(meta, [], own_w, (1, 0))
+    early_half = other_half(meta, [], own_w, (1,))
     partner, early_half = lax.optimization_barrier((partner, early_half))
     blocks = [jnp.where(first, tokens, partner), jnp.where(first, partner, tokens)]
     rows = blocks[0].shape[0] // 2
@@ -449,7 +471,10 @@
     starts = [lax.dynamic_slice_in_dim(block, mine * rows, rows, axis=0) for block in blocks]
     low_x, low_y, early_w = to_x(starts[0]), to_y(starts[0]), to_mod(early_half)
     low_x, low_y, start_high = lax.optimization_barrier((low_x, low_y, starts[1]))
-    late_w = to_mod(other_half(meta, [low_x, low_y], own_w, (2,)))
+    late_w = [
+        to_mod(other_half(meta, [starts[0]], own_w, (0,))),
+        to_mod(other_half(meta, [low_x, low_y], own_w, (2,))),
+    ]
     high_x, high_y = to_x(start_high), to_y(start_high)
     own_out = output_weight[0]
     arrived, projected = [], []
@@ -464,14 +489,15 @@
         arrived.append(lax.all_to_all(sent, "seq", 0, 0, tiled=True))
         projected.append(sent)
     low_mixed = attend(meta, projected[1], projected[1], arrived[0])
-    low_mixed, arrived[1] = lax.optimization_barrier((low_mixed, arrived[1]))
-    high_mixed = attend(meta, low_mixed, other_out, *arrived)
-
+    high_mixed = attend(meta, low_mixed[0], other_out, *arrived)
     results = []
     for chunk, mixed in enumerate((low_mixed, high_mixed)):
-        mixed = mixed.reshape((8,) + mixed.shape[2:])
-        heads = lax.all_to_all(mixed, ("mod", "seq"), 0, 0, tiled=True)
-        send_x, send_y, keep_a, keep_b = finish(chunk, meta, modality, results[-1] if chunk else high_mixed, heads, own_out, other_out)
+        far, mid, near = [lax.ppermute(mixed[k], "seq", swap(4, k)) for k in (3, 2, 1)]
+        heads = [mixed[0], near, mid, far]
+        cut = [lax.dynamic_slice_in_dim(head, (1 - mine) * rows, rows, axis=0) for head in heads]
+        heads.append(to_mod(jnp.stack(cut)))
+        after = send_x if chunk else high_mixed[0]
+        send_x, send_y, keep_a, keep_b = finish(chunk, meta, modality, after, heads, own_out, other_out)
         got_x, got_y = to_x(send_x).astype(jnp.float32), to_y(send_y).astype(jnp.float32)
         keep_a, keep_b = keep_a.astype(jnp.float32), keep_b.astype(jnp.float32)
         last_a = to_y((keep_a[1] + got_x[1]).astype(jnp.bfloat16)).astype(jnp.float32)

time: 254 us -> 229 us (0.902)
  waiting for transfers between devices: 111 us -> 101 us
  Pallas kernels: 88.8 us -> 78.9 us
  other arithmetic: 8.18 us -> 3.49 us
    all_to_all x2, waiting for transfers between devices: 47.7 us -> 1.77 us  [body(): arrived.append(lax.all_to_all(sent, 'seq', 0, 0, tiled=True))]
    ppermute x0 -> x6, waiting for transfers between devices: none -> 44.9 us  [body(): lax.ppermute(mixed[k], 'seq', swap(4, k))]
    ppermute x8, waiting for transfers between devices: 33 us -> 19.4 us  [to_y(): return lax.ppermute(value, 'tp', swap(4, 2))]
    ppermute x0 -> x6, starting transfers between devices: none -> 8.9 us  [body(): lax.ppermute(mixed[k], 'seq', swap(4, k))]
    all_to_all x2 -> x0, starting transfers between devices: 7.4 us -> none  [body(): heads = lax.all_to_all(mixed, ('mod', 'seq'), 0, 0, tiled=True)]
    ppermute x8, waiting for transfers between devices: 21.5 us -> 27 us  [to_x(): return lax.ppermute(value, 'tp', swap(4, 1))]
    pallas_call x2, Pallas kernels: 22.5 us -> 17.8 us  [finish(): pl.pallas_call(partial(finish_kernel, chunk), grid_spec=pltpu.PrefetchSca...]
    all_to_all x2 -> x0, waiting for transfers between devices: 4.5 us -> none  [body(): heads = lax.all_to_all(mixed, ('mod', 'seq'), 0, 0, tiled=True)]
  transfers between devices with their start and end apart: 27 -> 34, of which waited for: 19 -> 20; matrix products, arithmetic and copies ran while one was open for 3% -> 1% of each run, Pallas kernels for 26% -> 35%
where the time goes in v1:
time: 229 us; the launch traced here: 228 us
  waiting for transfers between devices  101 us (44%)
  Pallas kernels  78.9 us (34%)
  starting transfers between devices  36.2 us (16%)
  local copies, waits for them, and re-layouts  8 us (3%)
  other arithmetic  3.49 us (2%)
    ppermute x6, waiting for transfers between devices, body(): lax.ppermute(mixed[k], 'seq', swap(4, k))  44.9 us
    pallas_call x2, Pallas kernels, project(): pl.pallas_call(partial(project_kernel, chunk), in_specs=[scalars] * 2 + [...  38 us
    ppermute x8, waiting for transfers between devices, to_x(): return lax.ppermute(value, 'tp', swap(4, 1))  27 us
    ppermute x8, waiting for transfers between devices, to_y(): return lax.ppermute(value, 'tp', swap(4, 2))  19.4 us
    pallas_call x2, Pallas kernels, finish(): pl.pallas_call(partial(finish_kernel, chunk), grid_spec=pltpu.PrefetchSca...  17.8 us
    pallas_call x2, Pallas kernels, attend(): pl.pallas_call(partial(attend_kernel, high), in_specs=[pl.BlockSpec(memor...  13.6 us
    pallas_call x3, Pallas kernels, other_half(): pl.pallas_call(partial(half_kernel, parts), in_specs=[pl.BlockSpec(memory...  9.56 us
    ppermute x8, starting transfers between devices, to_y(): return lax.ppermute(value, 'tp', swap(4, 2))  9.51 us
  transfers between devices with their start and end apart: 34, of which 20 were waited for; matrix products, arithmetic and copies ran while one was open for 1% of the time, Pallas kernels for 35%

profile of v1, /device:TPU:0, one launch (start us, length us, event | category | flops | bytes accessed | tf_op | source)
XLA Modules:
  0.0 228.3 jit_solution(12565726699909975396)
XLA Ops:
  0.5 2.9 %other_half.3 = bf16[1,4096,512]{2,1,0:T(8,128)(2,1)S(1)} custom-call(s32[3]{0:T(128)S(1)} %pad_add_fusion.meta, bf16[3,4096,1024]{2,1,0:T(8,128)(2,1)} %bitcast.60), custom_call_target="tpu_custom_call" | custom-call | flops 4000000000 | bytes 1000 | tf_op jit(solution)/shard_map/other_half/pallas_call | solution.py:164
  3.6 2.6 %collective-permute-start.1 = (bf16[256,1024]{1,0:T(8,128)(2,1)S(1)}, bf16[256,1024]{1,0:T(8,128)(2,1)S(1)}, u32[]{:S(2)}, u32[]{:S(2)}) collective-permute-start(bf16[256,1024]{1,0:T(8,128)(2,1)S(1)} %constant_dynamic-slice_fusion.1.refs_0_), channel_id=1, source_target_pairs={{0,1},{1,0},{2,3},{3,2},{4,5},{5,4},{6,7},{7,6},{8,9},{9,8},{10,11... | collective-permute-start | bytes 1572872 | tf_op jit(solution)/shard_map/ppermute | solution.py:459
  6.2 1.5 collective-permute-start.2
  7.7 3.8 %other_half.4 = bf16[1,4096,512]{2,1,0:T(8,128)(2,1)} custom-call(s32[3]{0:T(128)S(1)} %pad_add_fusion.meta, bf16[3,4096,1024]{2,1,0:T(8,128)(2,1)} %bitcast.61, bf16[256,1024]{1,0:T(8,128)(2,1)S(1)} %constant_dynamic-slice_fusion.1.refs_0_), custom_call_target="tpu_custom_call" | custom-call | flops 4000000000 | bytes 1000 | tf_op jit(solution)/shard_map/other_half/pallas_call | solution.py:164
  12.2 6.6 %collective-permute-done.1.refs_0_.p1 = bf16[256,1024]{1,0:T(8,128)(2,1)S(1)} collective-permute-done((bf16[256,1024]{1,0:T(8,128)(2,1)S(1)}, bf16[256,1024]{1,0:T(8,128)(2,1)S(1)}, u32[]{:S(2)}, u32[]{:S(2)}) %collective-permute-start.1) | collective-permute-done | bytes 524320 | tf_op jit(solution)/shard_map/ppermute | solution.py:459
  18.8 1.5 collective-permute-done.2.refs_1_.p2
  20.2 2.9 %other_half.5 = bf16[1,4096,512]{2,1,0:T(8,128)(2,1)S(1)} custom-call(s32[3]{0:T(128)S(1)} %pad_add_fusion.meta, bf16[3,4096,1024]{2,1,0:T(8,128)(2,1)} %bitcast.62, bf16[256,1024]{1,0:T(8,128)(2,1)S(1)} %collective-permute-done.1.refs_0_.p1, bf16[256,1024]{1,0:T(8,128)(2,1)S(1)} %collective-permute-done.2.refs_1_.p2), custom_call_target="tpu_custom_call" | custom-call | flops 4000000000 | bytes 1000 | tf_op jit(solution)/shard_map/other_half/pallas_call | solution.py:164
  23.3 1.6 collective-permute-start.5
  25.4 6.6 %collective-permute-done.5.p3a = bf16[128,1024]{1,0:T(8,128)(2,1)S(1)} collective-permute-done((bf16[128,1024]{1,0:T(8,128)(2,1)S(1)}, bf16[128,1024]{1,0:T(8,128)(2,1)S(1)}, u32[]{:S(2)}, u32[]{:S(2)}) %collective-permute-start.5) | collective-permute-done | bytes 262176 | tf_op jit(solution)/shard_map/ppermute | solution.py:462
  32.0 1.2 collective-permute-done.6.p3b
  34.1 2.8 %collective-permute-done.7.q = bf16[768,1024]{1,0:T(8,128)(2,1)S(1)} collective-permute-done((bf16[768,1024]{1,0:T(8,128)(2,1)S(1)}, bf16[768,1024]{1,0:T(8,128)(2,1)S(1)}, u32[]{:S(2)}, u32[]{:S(2)}) %collective-permute-start.7) | collective-permute-done | bytes 1572896 | tf_op jit(solution)/shard_map/ppermute | solution.py:456
  37.5 19.8 %project.2 = bf16[4,3,512,128]{3,2,1,0:T(8,128)(2,1)} custom-call(s32[3]{0:T(128)S(1)} %pad_add_fusion.meta, s32[4096]{0:T(1024)S(1)} %copy-done.5, bf16[512,1024]{1,0:T(8,128)(2,1)S(1)} %get-tuple-element.53.block, bf16[256,1024]{1,0:T(8,128)(2,1)S(1)} %collective-permute-done.1.refs_0_.p1, bf16[256,1024]{1,0:T(8,128)(2,1)S(1)} %collective-permute-done.2.refs_1_.p2, ...), custom_call_target="tpu_custom_call" | custom-call | flops 1000 | bytes 1000 | tf_op jit(solution)/shard_map/project/pallas_call | solution.py:297
  57.4 4.9 %all-to-all-start = ((bf16[4,3,512,128]{3,2,1,0:T(8,128)(2,1)}), bf16[4,3,512,128]{3,2,1,0:T(8,128)(2,1)}, u32[]{:S(2)}, u32[]{:S(2)}) async-start(bf16[4,3,512,128]{3,2,1,0:T(8,128)(2,1)} %project.2), calls=%async_computation | async-start | bytes 3145728 | tf_op jit(solution)/shard_map/all_to_all | solution.py:489
  62.3 1.6 collective-permute-start.11
  64.5 6.3 %collective-permute-done.11.p3a = bf16[128,1024]{1,0:T(8,128)(2,1)S(1)} collective-permute-done((bf16[128,1024]{1,0:T(8,128)(2,1)S(1)}, bf16[128,1024]{1,0:T(8,128)(2,1)S(1)}, u32[]{:S(2)}, u32[]{:S(2)}) %collective-permute-start.11) | collective-permute-done | bytes 262176 | tf_op jit(solution)/shard_map/ppermute | solution.py:462
  70.8 1.3 collective-permute-done.12.p3b
  72.3 3.4 %collective-permute-done.13.q = bf16[768,1024]{1,0:T(8,128)(2,1)S(1)} collective-permute-done((bf16[768,1024]{1,0:T(8,128)(2,1)S(1)}, bf16[768,1024]{1,0:T(8,128)(2,1)S(1)}, u32[]{:S(2)}, u32[]{:S(2)}) %collective-permute-start.13) | collective-permute-done | bytes 1572896 | tf_op jit(solution)/shard_map/ppermute | solution.py:456
  75.7 2.2 copy-done.1
  77.9 2.2 copy-done.3
  80.1 18.1 %project.3.after.later = bf16[4,3,512,128]{3,2,1,0:T(8,128)(2,1)} custom-call(s32[3]{0:T(128)S(1)} %pad_add_fusion.meta, s32[4096]{0:T(1024)S(1)} %copy-done.5, bf16[512,1024]{1,0:T(8,128)(2,1)S(1)} %get-tuple-element.54.block, bf16[256,1024]{1,0:T(8,128)(2,1)S(1)} %collective-permute-done.3.p1, bf16[256,1024]{1,0:T(8,128)(2,1)S(1)} %collective-permute-done.4.p2, ...), custom_call_target="tpu_custom_call" | custom-call | flops 1000 | bytes 1000 | tf_op jit(solution)/shard_map/project/pallas_call | solution.py:297
  98.2 1.8 all-to-all-done.refs_0_
  100.0 3.7 %all-to-all-start.1 = ((bf16[4,3,512,128]{3,2,1,0:T(8,128)(2,1)}), bf16[4,3,512,128]{3,2,1,0:T(8,128)(2,1)S(1)}, u32[]{:S(2)}, u32[]{:S(2)}) async-start(bf16[4,3,512,128]{3,2,1,0:T(8,128)(2,1)} %project.3.after.later), calls=%async_computation.1 | async-start | bytes 3145728 | tf_op jit(solution)/shard_map/all_to_all | solution.py:489
  103.8 4.5 %attend.2 = (bf16[512,128]{1,0:T(8,128)(2,1)S(1)}, bf16[512,128]{1,0:T(8,128)(2,1)S(1)}, bf16[512,128]{1,0:T(8,128)(2,1)S(1)}, bf16[512,128]{1,0:T(8,128)(2,1)S(1)}) custom-call(s32[3]{0:T(128)S(1)} %pad_add_fusion.meta, bf16[4,3,512,128]{3,2,1,0:T(8,128)(2,1)} %project.3.after.later, bf16[4,3,512,128]{3,2,1,0:T(8,128)(2,1)} %project.3.after.later, ...), custom_call_target="tpu_custom_call" | custom-call | flops 6000000000 | bytes 1000 | tf_op jit(solution)/shard_map/attend/pallas_call | solution.py:362
  108.3 3.7 %collective-permute-start.17 = (bf16[512,128]{1,0:T(8,128)(2,1)S(1)}, bf16[512,128]{1,0:T(8,128)(2,1)S(1)}, u32[]{:S(2)}, u32[]{:S(2)}) collective-permute-start(bf16[512,128]{1,0:T(8,128)(2,1)S(1)} %get-tuple-element.41), channel_id=1, source_target_pairs={{0,12},{4,8},{8,4},{12,0},{1,13},{5,9},{9,5},{13,1},{2,14},{6,10},... | collective-permute-start | bytes 393224 | tf_op jit(solution)/shard_map/ppermute | solution.py:495
  112.0 0.8 collective-permute-start.15
  112.8 24.6 %collective-permute-done.17.refs_3_ = bf16[512,128]{1,0:T(8,128)(2,1)S(1)} collective-permute-done((bf16[512,128]{1,0:T(8,128)(2,1)S(1)}, bf16[512,128]{1,0:T(8,128)(2,1)S(1)}, u32[]{:S(2)}, u32[]{:S(2)}) %collective-permute-start.17) | collective-permute-done | bytes 131104 | tf_op jit(solution)/shard_map/ppermute | solution.py:495
  137.3 14.3 %collective-permute-done.16.refs_2_ = bf16[512,128]{1,0:T(8,128)(2,1)S(1)} collective-permute-done((bf16[512,128]{1,0:T(8,128)(2,1)S(1)}, bf16[512,128]{1,0:T(8,128)(2,1)S(1)}, u32[]{:S(2)}, u32[]{:S(2)}) %collective-permute-start.16) | collective-permute-done | bytes 131104 | tf_op jit(solution)/shard_map/ppermute | solution.py:495
  151.8 9.1 %attend.3 = (bf16[512,128]{1,0:T(8,128)(2,1)S(1)}, bf16[512,128]{1,0:T(8,128)(2,1)S(1)}, bf16[512,128]{1,0:T(8,128)(2,1)S(1)}, bf16[512,128]{1,0:T(8,128)(2,1)S(1)}) custom-call(s32[3]{0:T(128)S(1)} %pad_add_fusion.meta, bf16[512,128]{1,0:T(8,128)(2,1)S(1)} %get-tuple-element.36.after.refs_0_, bf16[1024,4096]{1,0:T(8,128)(2,1)} %collective-permute-done.14.later.refs_6_, ...), custom_call_target="tpu_custom_call" | custom-call | flops 12000000000 | bytes 1000 | tf_op jit(solution)/shard_map/attend/pallas_call | solution.py:362
  160.8 1.5 collective-permute-start.25
  162.4 3.4 %copy-done.7 = bf16[1,1024,4096]{2,1,0:T(8,128)(2,1)S(1)} copy-done((bf16[1,1024,4096]{2,1,0:T(8,128)(2,1)S(1)}, bf16[1,1024,4096]{2,1,0:T(8,128)(2,1)}, u32[]{:S(2)}) %copy-start.7) | copy-done | bytes 8388632
  165.8 9.0 %finish.2 = (bf16[2,128,1024]{2,1,0:T(8,128)(2,1)S(1)}, bf16[2,128,1024]{2,1,0:T(8,128)(2,1)S(1)}, bf16[2,128,1024]{2,1,0:T(8,128)(2,1)S(1)}, bf16[2,128,1024]{2,1,0:T(8,128)(2,1)S(1)}) custom-call(s32[3]{0:T(128)S(1)} %pad_add_fusion.meta, s32[4096]{0:T(1024)S(1)} %copy-done.5, bf16[512,128]{1,0:T(8,128)(2,1)S(1)} %get-tuple-element.38.after.refs_0_, ...), custom_call_target="tpu_custom_call" | custom-call | flops 12000000000 | bytes 1000 | tf_op jit(solution)/shard_map/finish/pallas_call | solution.py:430
  174.8 0.6 collective-permute-start.19
  175.4 2.9 %collective-permute-start.23 = (bf16[512,128]{1,0:T(8,128)(2,1)S(1)}, bf16[512,128]{1,0:T(8,128)(2,1)S(1)}, u32[]{:S(2)}, u32[]{:S(2)}) collective-permute-start(bf16[512,128]{1,0:T(8,128)(2,1)S(1)} %get-tuple-element.46), channel_id=1, source_target_pairs={{0,4},{4,0},{8,12},{12,8},{1,5},{5,1},{9,13},{13,9},{2,6},{6,2},{1... | collective-permute-start | bytes 393224 | tf_op jit(solution)/shard_map/ppermute | solution.py:495
  178.4 5.9 %collective-permute-done.24.refs_2_ = bf16[512,128]{1,0:T(8,128)(2,1)S(1)} collective-permute-done((bf16[512,128]{1,0:T(8,128)(2,1)S(1)}, bf16[512,128]{1,0:T(8,128)(2,1)S(1)}, u32[]{:S(2)}, u32[]{:S(2)}) %collective-permute-start.24) | collective-permute-done | bytes 131104 | tf_op jit(solution)/shard_map/ppermute | solution.py:495
  184.7 1.6 collective-permute-start.21
  186.3 2.6 %collective-permute-done.19 = bf16[2,128,1024]{2,1,0:T(8,128)(2,1)S(1)} collective-permute-done((bf16[2,128,1024]{2,1,0:T(8,128)(2,1)S(1)}, bf16[2,128,1024]{2,1,0:T(8,128)(2,1)S(1)}, u32[]{:S(2)}, u32[]{:S(2)}) %collective-permute-start.19) | collective-permute-done | bytes 524320 | tf_op jit(solution)/shard_map/ppermute | solution.py:459
  189.1 1.6 collective-permute-start.20
  190.7 8.7 %finish.3 = (bf16[2,128,1024]{2,1,0:T(8,128)(2,1)S(1)}, bf16[2,128,1024]{2,1,0:T(8,128)(2,1)S(1)}, bf16[2,128,1024]{2,1,0:T(8,128)(2,1)S(1)}, bf16[2,128,1024]{2,1,0:T(8,128)(2,1)S(1)}) custom-call(s32[3]{0:T(128)S(1)} %pad_add_fusion.meta, s32[4096]{0:T(1024)S(1)} %copy-done.5, bf16[2,128,1024]{2,1,0:T(8,128)(2,1)S(1)} %get-tuple-element.43.after, ...), custom_call_target="tpu_custom_call" | custom-call | flops 12000000000 | bytes 1000 | tf_op jit(solution)/shard_map/finish/pallas_call | solution.py:430
  199.4 0.6 collective-permute-start.27
  201.1 1.5 collective-permute-start.22
  202.7 2.4 %collective-permute-done.20 = bf16[128,1024]{1,0:T(8,128)(2,1)S(1)} collective-permute-done((bf16[128,1024]{1,0:T(8,128)(2,1)S(1)}, bf16[128,1024]{1,0:T(8,128)(2,1)S(1)}, u32[]{:S(2)}, u32[]{:S(2)}) %collective-permute-start.20) | collective-permute-done | bytes 262176 | tf_op jit(solution)/shard_map/ppermute | solution.py:462
  205.2 9.2 %collective-permute-done.27 = bf16[2,128,1024]{2,1,0:T(8,128)(2,1)S(1)} collective-permute-done((bf16[2,128,1024]{2,1,0:T(8,128)(2,1)S(1)}, bf16[2,128,1024]{2,1,0:T(8,128)(2,1)S(1)}, u32[]{:S(2)}, u32[]{:S(2)}) %collective-permute-start.27) | collective-permute-done | bytes 524320 | tf_op jit(solution)/shard_map/ppermute | solution.py:459
  215.1 2.9 %collective-permute-done.22 = bf16[128,1024]{1,0:T(8,128)(2,1)S(1)} collective-permute-done((bf16[128,1024]{1,0:T(8,128)(2,1)S(1)}, bf16[128,1024]{1,0:T(8,128)(2,1)S(1)}, u32[]{:S(2)}, u32[]{:S(2)}) %collective-permute-start.22) | collective-permute-done | bytes 262176 | tf_op jit(solution)/shard_map/ppermute | solution.py:459
  218.3 0.6 collective-permute-start.30
  218.9 2.6 %collective-permute-done.28 = bf16[128,1024]{1,0:T(8,128)(2,1)S(1)} collective-permute-done((bf16[128,1024]{1,0:T(8,128)(2,1)S(1)}, bf16[128,1024]{1,0:T(8,128)(2,1)S(1)}, u32[]{:S(2)}, u32[]{:S(2)}) %collective-permute-start.28) | collective-permute-done | bytes 262176 | tf_op jit(solution)/shard_map/ppermute | solution.py:462
  221.6 3.1 %collective-permute-done.30 = bf16[128,1024]{1,0:T(8,128)(2,1)S(1)} collective-permute-done((bf16[128,1024]{1,0:T(8,128)(2,1)S(1)}, bf16[128,1024]{1,0:T(8,128)(2,1)S(1)}, u32[]{:S(2)}, u32[]{:S(2)}) %collective-permute-start.30) | collective-permute-done | bytes 262176 | tf_op jit(solution)/shard_map/ppermute | solution.py:459
  225.1 1.9 collective-permute-done.31
  227.3 1.0 pad_maximum_fusion.2
  (91 shorter events, 7.9 us)
Async XLA Ops:
  0.0 3.4 %collective-permute-start = (bf16[512,1024]{1,0:T(8,128)(2,1)}, bf16[512,1024]{1,0:T(8,128)(2,1)S(1)}, u32[]{:S(2)}, u32[]{:S(2)}) collective-permute-start(bf16[512,1024]{1,0:T(8,128)(2,1)} %param.6), channel_id=1, source_target_pairs={{0,16},{16,0},{1,17},{17,1},{2,18},{18,2},{3,19},{19,3},{4,20},{20... | collective-permute-start | bytes 3145736 | tf_op jit(solution)/shard_map/ppermute | solution.py:456
  0.5 2.9 %copy-start.8 = (bf16[512,1024]{1,0:T(8,128)(2,1)S(1)}, bf16[512,1024]{1,0:T(8,128)(2,1)}, u32[]{:S(2)}) copy-start(bf16[512,1024]{1,0:T(8,128)(2,1)} %param.6) | copy-start | bytes 3145732
  3.6 15.2 %collective-permute-start.1 = (bf16[256,1024]{1,0:T(8,128)(2,1)S(1)}, bf16[256,1024]{1,0:T(8,128)(2,1)S(1)}, u32[]{:S(2)}, u32[]{:S(2)}) collective-permute-start(bf16[256,1024]{1,0:T(8,128)(2,1)S(1)} %constant_dynamic-slice_fusion.1.refs_0_), channel_id=1, source_target_pairs={{0,1},{1,0},{2,3},{3,2},{4,5},{5,4},{6,7},{7,6},{8,9},{9,8},{10,11... | collective-permute-start | bytes 1572872 | tf_op jit(solution)/shard_map/ppermute | solution.py:459
  6.2 14.1 %collective-permute-start.2 = (bf16[256,1024]{1,0:T(8,128)(2,1)S(1)}, bf16[256,1024]{1,0:T(8,128)(2,1)S(1)}, u32[]{:S(2)}, u32[]{:S(2)}) collective-permute-start(bf16[256,1024]{1,0:T(8,128)(2,1)S(1)} %constant_dynamic-slice_fusion.1.refs_0_), channel_id=1, source_target_pairs={{0,2},{1,3},{2,0},{3,1},{4,6},{5,7},{6,4},{7,5},{8,10},{9,11},{10,... | collective-permute-start | bytes 1572872 | tf_op jit(solution)/shard_map/ppermute | solution.py:462
  11.5 25.9 %collective-permute-start.9 = (bf16[1,4096,512]{2,1,0:T(8,128)(2,1)}, bf16[1,4096,512]{2,1,0:T(8,128)(2,1)S(1)}, u32[]{:S(2)}, u32[]{:S(2)}) collective-permute-start(bf16[1,4096,512]{2,1,0:T(8,128)(2,1)} %other_half.4), channel_id=1, source_target_pairs={{0,16},{16,0},{1,17},{17,1},{2,18},{18,2},{3,19},{19,3},{4,20},{20... | collective-permute-start | bytes 12582920 | tf_op jit(solution)/shard_map/ppermute | solution.py:456
  11.6 25.8 %collective-permute-start.8 = (bf16[1,4096,512]{2,1,0:T(8,128)(2,1)S(1)}, bf16[1,4096,512]{2,1,0:T(8,128)(2,1)S(1)}, u32[]{:S(2)}, u32[]{:S(2)}) collective-permute-start(bf16[1,4096,512]{2,1,0:T(8,128)(2,1)S(1)} %other_half.3), channel_id=1, source_target_pairs={{0,16},{16,0},{1,17},{17,1},{2,18},{18,2},{3,19},{19,3},{4,20},{20... | collective-permute-start | bytes 12582920 | tf_op jit(solution)/shard_map/ppermute | solution.py:456
  23.1 14.3 %copy-start.4 = (f32[2,4096]{1,0:T(2,128)S(1)}, f32[2,4096]{1,0:T(2,128)}, u32[]{:S(2)}) copy-start(f32[2,4096]{1,0:T(2,128)} %gain.3) | copy-start | bytes 98308
  23.1 14.3 %copy-start.5 = (s32[4096]{0:T(1024)S(1)}, s32[4096]{0:T(1024)}, u32[]{:S(2)}) copy-start(s32[4096]{0:T(1024)} %ids.7) | copy-start | bytes 49156
  23.1 14.3 %copy-start.6 = (f32[2,2,128]{2,1,0:T(2,128)S(1)}, f32[2,2,128]{2,1,0:T(2,128)}, u32[]{:S(2)}) copy-start(f32[2,2,128]{2,1,0:T(2,128)} %head_gain.3) | copy-start | bytes 6148
  23.1 14.3 %collective-permute-start.10 = (bf16[1,4096,512]{2,1,0:T(8,128)(2,1)S(1)}, bf16[1,4096,512]{2,1,0:T(8,128)(2,1)}, u32[]{:S(2)}, u32[]{:S(2)}) collective-permute-start(bf16[1,4096,512]{2,1,0:T(8,128)(2,1)S(1)} %other_half.5), channel_id=1, source_target_pairs={{0,16},{16,0},{1,17},{17,1},{2,18},{18,2},{3,19},{19,3},{4,20},{20... | collective-permute-start | bytes 12582920 | tf_op jit(solution)/shard_map/ppermute | solution.py:456
  23.3 8.8 %collective-permute-start.5 = (bf16[128,1024]{1,0:T(8,128)(2,1)S(1)}, bf16[128,1024]{1,0:T(8,128)(2,1)S(1)}, u32[]{:S(2)}, u32[]{:S(2)}) collective-permute-start(bf16[128,1024]{1,0:T(8,128)(2,1)S(1)} %slice.60), channel_id=1, source_target_pairs={{0,2},{1,3},{2,0},{3,1},{4,6},{5,7},{6,4},{7,5},{8,10},{9,11},{10,... | collective-permute-start | bytes 786440 | tf_op jit(solution)/shard_map/ppermute | solution.py:462
  24.9 8.4 %collective-permute-start.6 = (bf16[128,1024]{1,0:T(8,128)(2,1)S(1)}, bf16[128,1024]{1,0:T(8,128)(2,1)S(1)}, u32[]{:S(2)}, u32[]{:S(2)}) collective-permute-start(bf16[128,1024]{1,0:T(8,128)(2,1)S(1)} %slice.61), channel_id=1, source_target_pairs={{0,1},{1,0},{2,3},{3,2},{4,5},{5,4},{6,7},{7,6},{8,9},{9,8},{10,11... | collective-permute-start | bytes 786440 | tf_op jit(solution)/shard_map/ppermute | solution.py:459
  33.4 3.5 %collective-permute-start.7 = (bf16[768,1024]{1,0:T(8,128)(2,1)S(1)}, bf16[768,1024]{1,0:T(8,128)(2,1)S(1)}, u32[]{:S(2)}, u32[]{:S(2)}) collective-permute-start(bf16[768,1024]{1,0:T(8,128)(2,1)S(1)} %pad_maximum_fusion), channel_id=1, source_target_pairs={{0,16},{16,0},{1,17},{17,1},{2,18},{18,2},{3,19},{19,3},{4,20},{20... | collective-permute-start | bytes 4718600 | tf_op jit(solution)/shard_map/ppermute | solution.py:456
  33.5 23.8 %collective-permute-start.3 = (bf16[256,1024]{1,0:T(8,128)(2,1)S(1)}, bf16[256,1024]{1,0:T(8,128)(2,1)S(1)}, u32[]{:S(2)}, u32[]{:S(2)}) collective-permute-start(bf16[256,1024]{1,0:T(8,128)(2,1)S(1)} %constant_dynamic-slice_fusion), channel_id=1, source_target_pairs={{0,1},{1,0},{2,3},{3,2},{4,5},{5,4},{6,7},{7,6},{8,9},{9,8},{10,11... | collective-permute-start | bytes 1572872 | tf_op jit(solution)/shard_map/ppermute | solution.py:459
  36.9 20.4 %collective-permute-start.4 = (bf16[256,1024]{1,0:T(8,128)(2,1)S(1)}, bf16[256,1024]{1,0:T(8,128)(2,1)S(1)}, u32[]{:S(2)}, u32[]{:S(2)}) collective-permute-start(bf16[256,1024]{1,0:T(8,128)(2,1)S(1)} %constant_dynamic-slice_fusion), channel_id=1, source_target_pairs={{0,2},{1,3},{2,0},{3,1},{4,6},{5,7},{6,4},{7,5},{8,10},{9,11},{10,... | collective-permute-start | bytes 1572872 | tf_op jit(solution)/shard_map/ppermute | solution.py:462
  37.4 19.9 %copy-start = (bf16[1,4096,512]{2,1,0:T(8,128)(2,1)}, bf16[1,4096,512]{2,1,0:T(8,128)(2,1)S(1)}, u32[]{:S(2)}) copy-start(bf16[1,4096,512]{2,1,0:T(8,128)(2,1)S(1)} %collective-permute-done.9.query_w) | copy-start | bytes 12582916
  37.4 19.9 %copy-start.2 = (bf16[1,4096,512]{2,1,0:T(8,128)(2,1)}, bf16[1,4096,512]{2,1,0:T(8,128)(2,1)S(1)}, u32[]{:S(2)}) copy-start(bf16[1,4096,512]{2,1,0:T(8,128)(2,1)S(1)} %collective-permute-done.8.early_w) | copy-start | bytes 12582916
  57.3 94.4 %collective-permute-start.14 = (bf16[1024,4096]{1,0:T(8,128)(2,1)}, bf16[1024,4096]{1,0:T(8,128)(2,1)}, u32[]{:S(2)}, u32[]{:S(2)}) collective-permute-start(bf16[1024,4096]{1,0:T(8,128)(2,1)} %bitcast.55), channel_id=1, source_target_pairs={{0,16},{16,0},{1,17},{17,1},{2,18},{18,2},{3,19},{19,3},{4,20},{20... | collective-permute-start | bytes 25165832 | tf_op jit(solution)/shard_map/ppermute | solution.py:456
  57.4 42.6 %all-to-all-start = ((bf16[4,3,512,128]{3,2,1,0:T(8,128)(2,1)}), bf16[4,3,512,128]{3,2,1,0:T(8,128)(2,1)}, u32[]{:S(2)}, u32[]{:S(2)}) async-start(bf16[4,3,512,128]{3,2,1,0:T(8,128)(2,1)} %project.2), calls=%async_computation | async-start | bytes 3145728 | tf_op jit(solution)/shard_map/all_to_all | solution.py:489
  62.3 8.5 %collective-permute-start.11 = (bf16[128,1024]{1,0:T(8,128)(2,1)S(1)}, bf16[128,1024]{1,0:T(8,128)(2,1)S(1)}, u32[]{:S(2)}, u32[]{:S(2)}) collective-permute-start(bf16[128,1024]{1,0:T(8,128)(2,1)S(1)} %slice.62), channel_id=1, source_target_pairs={{0,2},{1,3},{2,0},{3,1},{4,6},{5,7},{6,4},{7,5},{8,10},{9,11},{10,... | collective-permute-start | bytes 786440 | tf_op jit(solution)/shard_map/ppermute | solution.py:462
  63.9 8.2 %collective-permute-start.12 = (bf16[128,1024]{1,0:T(8,128)(2,1)S(1)}, bf16[128,1024]{1,0:T(8,128)(2,1)S(1)}, u32[]{:S(2)}, u32[]{:S(2)}) collective-permute-start(bf16[128,1024]{1,0:T(8,128)(2,1)S(1)} %slice.63), channel_id=1, source_target_pairs={{0,1},{1,0},{2,3},{3,2},{4,5},{5,4},{6,7},{7,6},{8,9},{9,8},{10,11... | collective-permute-start | bytes 786440 | tf_op jit(solution)/shard_map/ppermute | solution.py:459
  72.2 3.5 %collective-permute-start.13 = (bf16[768,1024]{1,0:T(8,128)(2,1)S(1)}, bf16[768,1024]{1,0:T(8,128)(2,1)S(1)}, u32[]{:S(2)}, u32[]{:S(2)}) collective-permute-start(bf16[768,1024]{1,0:T(8,128)(2,1)S(1)} %pad_maximum_fusion.1), channel_id=1, source_target_pairs={{0,16},{16,0},{1,17},{17,1},{2,18},{18,2},{3,19},{19,3},{4,20},{20... | collective-permute-start | bytes 4718600 | tf_op jit(solution)/shard_map/ppermute | solution.py:456
  75.7 2.2 copy-start.1
  77.9 2.2 copy-start.3
  100.0 51.7 %all-to-all-start.1 = ((bf16[4,3,512,128]{3,2,1,0:T(8,128)(2,1)}), bf16[4,3,512,128]{3,2,1,0:T(8,128)(2,1)S(1)}, u32[]{:S(2)}, u32[]{:S(2)}) async-start(bf16[4,3,512,128]{3,2,1,0:T(8,128)(2,1)} %project.3.after.later), calls=%async_computation.1 | async-start | bytes 3145728 | tf_op jit(solution)/shard_map/all_to_all | solution.py:489
  108.3 29.0 %collective-permute-start.17 = (bf16[512,128]{1,0:T(8,128)(2,1)S(1)}, bf16[512,128]{1,0:T(8,128)(2,1)S(1)}, u32[]{:S(2)}, u32[]{:S(2)}) collective-permute-start(bf16[512,128]{1,0:T(8,128)(2,1)S(1)} %get-tuple-element.41), channel_id=1, source_target_pairs={{0,12},{4,8},{8,4},{12,0},{1,13},{5,9},{9,5},{13,1},{2,14},{6,10},... | collective-permute-start | bytes 393224 | tf_op jit(solution)/shard_map/ppermute | solution.py:495
  112.0 39.6 %collective-permute-start.16 = (bf16[512,128]{1,0:T(8,128)(2,1)S(1)}, bf16[512,128]{1,0:T(8,128)(2,1)S(1)}, u32[]{:S(2)}, u32[]{:S(2)}) collective-permute-start(bf16[512,128]{1,0:T(8,128)(2,1)S(1)} %get-tuple-element.40), channel_id=1, source_target_pairs={{0,8},{4,12},{8,0},{12,4},{1,9},{5,13},{9,1},{13,5},{2,10},{6,14},... | collective-permute-start | bytes 393224 | tf_op jit(solution)/shard_map/ppermute | solution.py:495
  112.0 39.6 %collective-permute-start.15 = (bf16[512,128]{1,0:T(8,128)(2,1)S(1)}, bf16[512,128]{1,0:T(8,128)(2,1)S(1)}, u32[]{:S(2)}, u32[]{:S(2)}) collective-permute-start(bf16[512,128]{1,0:T(8,128)(2,1)S(1)} %get-tuple-element.39), channel_id=1, source_target_pairs={{0,4},{4,0},{8,12},{12,8},{1,5},{5,1},{9,13},{13,9},{2,6},{6,2},{1... | collective-permute-start | bytes 393224 | tf_op jit(solution)/shard_map/ppermute | solution.py:495
  151.7 10.7 %collective-permute-start.18 = (bf16[4,256,128]{2,1,0:T(8,128)(2,1)S(1)}, bf16[4,256,128]{2,1,0:T(8,128)(2,1)S(1)}, u32[]{:S(2)}, u32[]{:S(2)}) collective-permute-start(bf16[4,256,128]{2,1,0:T(8,128)(2,1)S(1)} %pad_maximum_fusion.5), channel_id=1, source_target_pairs={{0,16},{16,0},{1,17},{17,1},{2,18},{18,2},{3,19},{19,3},{4,20},{20... | collective-permute-start | bytes 786440 | tf_op jit(solution)/shard_map/ppermute | solution.py:456
  151.8 38.9 %slice-start = ((s8[8388608]{0:T(1024)(128)(4,1)}), s8[4194304]{0:T(1024)(128)(4,1)S(1)}, s32[]{:S(2)}) async-start(s8[8388608]{0:T(1024)(128)(4,1)} %bitcast.57), calls=%async_computation.2 | async-start | bytes 8388608
  160.8 17.5 %collective-permute-start.25 = (bf16[512,128]{1,0:T(8,128)(2,1)S(1)}, bf16[512,128]{1,0:T(8,128)(2,1)S(1)}, u32[]{:S(2)}, u32[]{:S(2)}) collective-permute-start(bf16[512,128]{1,0:T(8,128)(2,1)S(1)} %get-tuple-element.48), channel_id=1, source_target_pairs={{0,12},{4,8},{8,4},{12,0},{1,13},{5,9},{9,5},{13,1},{2,14},{6,10},... | collective-permute-start | bytes 393224 | tf_op jit(solution)/shard_map/ppermute | solution.py:495
  162.4 3.4 %copy-start.7 = (bf16[1,1024,4096]{2,1,0:T(8,128)(2,1)S(1)}, bf16[1,1024,4096]{2,1,0:T(8,128)(2,1)}, u32[]{:S(2)}) copy-start(bf16[1,1024,4096]{2,1,0:T(8,128)(2,1)} %param.11) | copy-start | bytes 25165828
  165.8 24.9 %slice-start.1 = ((s8[8388608]{0:T(1024)(128)(4,1)}), s8[4194304]{0:T(1024)(128)(4,1)S(1)}, s32[]{:S(2)}) async-start(s8[8388608]{0:T(1024)(128)(4,1)} %bitcast.57), calls=%async_computation.3 | async-start | bytes 8388608
  174.8 14.1 %collective-permute-start.19 = (bf16[2,128,1024]{2,1,0:T(8,128)(2,1)S(1)}, bf16[2,128,1024]{2,1,0:T(8,128)(2,1)S(1)}, u32[]{:S(2)}, u32[]{:S(2)}) collective-permute-start(bf16[2,128,1024]{2,1,0:T(8,128)(2,1)S(1)} %get-tuple-element.43.after), channel_id=1, source_target_pairs={{0,1},{1,0},{2,3},{3,2},{4,5},{5,4},{6,7},{7,6},{8,9},{9,8},{10,11... | collective-permute-start | bytes 1572872 | tf_op jit(solution)/shard_map/ppermute | solution.py:459
  175.4 8.9 %collective-permute-start.24 = (bf16[512,128]{1,0:T(8,128)(2,1)S(1)}, bf16[512,128]{1,0:T(8,128)(2,1)S(1)}, u32[]{:S(2)}, u32[]{:S(2)}) collective-permute-start(bf16[512,128]{1,0:T(8,128)(2,1)S(1)} %get-tuple-element.47), channel_id=1, source_target_pairs={{0,8},{4,12},{8,0},{12,4},{1,9},{5,13},{9,1},{13,5},{2,10},{6,14},... | collective-permute-start | bytes 393224 | tf_op jit(solution)/shard_map/ppermute | solution.py:495
  175.4 9.0 %collective-permute-start.23 = (bf16[512,128]{1,0:T(8,128)(2,1)S(1)}, bf16[512,128]{1,0:T(8,128)(2,1)S(1)}, u32[]{:S(2)}, u32[]{:S(2)}) collective-permute-start(bf16[512,128]{1,0:T(8,128)(2,1)S(1)} %get-tuple-element.46), channel_id=1, source_target_pairs={{0,4},{4,0},{8,12},{12,8},{1,5},{5,1},{9,13},{13,9},{2,6},{6,2},{1... | collective-permute-start | bytes 393224 | tf_op jit(solution)/shard_map/ppermute | solution.py:495
  184.5 6.1 %collective-permute-start.26 = (bf16[4,256,128]{2,1,0:T(8,128)(2,1)S(1)}, bf16[4,256,128]{2,1,0:T(8,128)(2,1)S(1)}, u32[]{:S(2)}, u32[]{:S(2)}) collective-permute-start(bf16[4,256,128]{2,1,0:T(8,128)(2,1)S(1)} %pad_maximum_fusion.6), channel_id=1, source_target_pairs={{0,16},{16,0},{1,17},{17,1},{2,18},{18,2},{3,19},{19,3},{4,20},{20... | collective-permute-start | bytes 786440 | tf_op jit(solution)/shard_map/ppermute | solution.py:456
  184.7 16.3 %collective-permute-start.21 = (bf16[2,128,1024]{2,1,0:T(8,128)(2,1)S(1)}, bf16[2,128,1024]{2,1,0:T(8,128)(2,1)S(1)}, u32[]{:S(2)}, u32[]{:S(2)}) collective-permute-start(bf16[2,128,1024]{2,1,0:T(8,128)(2,1)S(1)} %get-tuple-element.45), channel_id=1, source_target_pairs={{0,2},{1,3},{2,0},{3,1},{4,6},{5,7},{6,4},{7,5},{8,10},{9,11},{10,... | collective-permute-start | bytes 1572872 | tf_op jit(solution)/shard_map/ppermute | solution.py:462
  189.1 16.0 %collective-permute-start.20 = (bf16[128,1024]{1,0:T(8,128)(2,1)S(1)}, bf16[128,1024]{1,0:T(8,128)(2,1)S(1)}, u32[]{:S(2)}, u32[]{:S(2)}) collective-permute-start(bf16[128,1024]{1,0:T(8,128)(2,1)S(1)} %fusion.16), channel_id=1, source_target_pairs={{0,2},{1,3},{2,0},{3,1},{4,6},{5,7},{6,4},{7,5},{8,10},{9,11},{10,... | collective-permute-start | bytes 786440 | tf_op jit(solution)/shard_map/ppermute | solution.py:462
  199.4 14.9 %collective-permute-start.27 = (bf16[2,128,1024]{2,1,0:T(8,128)(2,1)S(1)}, bf16[2,128,1024]{2,1,0:T(8,128)(2,1)S(1)}, u32[]{:S(2)}, u32[]{:S(2)}) collective-permute-start(bf16[2,128,1024]{2,1,0:T(8,128)(2,1)S(1)} %get-tuple-element.50), channel_id=1, source_target_pairs={{0,1},{1,0},{2,3},{3,2},{4,5},{5,4},{6,7},{7,6},{8,9},{9,8},{10,11... | collective-permute-start | bytes 1572872 | tf_op jit(solution)/shard_map/ppermute | solution.py:459
  200.2 17.9 %collective-permute-start.29 = (bf16[2,128,1024]{2,1,0:T(8,128)(2,1)S(1)}, bf16[2,128,1024]{2,1,0:T(8,128)(2,1)S(1)}, u32[]{:S(2)}, u32[]{:S(2)}) collective-permute-start(bf16[2,128,1024]{2,1,0:T(8,128)(2,1)S(1)} %get-tuple-element.52), channel_id=1, source_target_pairs={{0,2},{1,3},{2,0},{3,1},{4,6},{5,7},{6,4},{7,5},{8,10},{9,11},{10,... | collective-permute-start | bytes 1572872 | tf_op jit(solution)/shard_map/ppermute | solution.py:462
  201.1 16.9 %collective-permute-start.22 = (bf16[128,1024]{1,0:T(8,128)(2,1)S(1)}, bf16[128,1024]{1,0:T(8,128)(2,1)S(1)}, u32[]{:S(2)}, u32[]{:S(2)}) collective-permute-start(bf16[128,1024]{1,0:T(8,128)(2,1)S(1)} %fusion.17), channel_id=1, source_target_pairs={{0,1},{1,0},{2,3},{3,2},{4,5},{5,4},{6,7},{7,6},{8,9},{9,8},{10,11... | collective-permute-start | bytes 786440 | tf_op jit(solution)/shard_map/ppermute | solution.py:459
  214.5 7.0 %collective-permute-start.28 = (bf16[128,1024]{1,0:T(8,128)(2,1)S(1)}, bf16[128,1024]{1,0:T(8,128)(2,1)S(1)}, u32[]{:S(2)}, u32[]{:S(2)}) collective-permute-start(bf16[128,1024]{1,0:T(8,128)(2,1)S(1)} %fusion.18), channel_id=1, source_target_pairs={{0,2},{1,3},{2,0},{3,1},{4,6},{5,7},{6,4},{7,5},{8,10},{9,11},{10,... | collective-permute-start | bytes 786440 | tf_op jit(solution)/shard_map/ppermute | solution.py:462
  218.3 6.4 %collective-permute-start.30 = (bf16[128,1024]{1,0:T(8,128)(2,1)S(1)}, bf16[128,1024]{1,0:T(8,128)(2,1)S(1)}, u32[]{:S(2)}, u32[]{:S(2)}) collective-permute-start(bf16[128,1024]{1,0:T(8,128)(2,1)S(1)} %fusion.19), channel_id=1, source_target_pairs={{0,1},{1,0},{2,3},{3,2},{4,5},{5,4},{6,7},{7,6},{8,9},{9,8},{10,11... | collective-permute-start | bytes 786440 | tf_op jit(solution)/shard_map/ppermute | solution.py:459
  225.0 2.0 collective-permute-start.31
